TPU v7x, 128 devices: a whole 4x4x4 slice. The times are simulated.
128 devices in a mesh: gx: 8 (over x, core), gy: 16 (over z, y).
Axes of the slice: x: 4, y: 4, z: 4, core: 2. Of those that a mesh axis runs over, the one named last changes fastest.
Arguments:
- flow: float32 [5, 128, 512, 128], P(None, 'gx', 'gy'), may hold values from -6 to 6
- near: float32 [5, 16384], P(None, ('gx', 'gy')), may hold values from -6 to 6
- donor_owner: int32 [16384, 1], P(('gx', 'gy')), may hold values from 0 to 127; in each aligned block of 128 rows (0 to 127, 128 to 255, ...) at most 2 rows name the same one
- donor_block: int32 [16384], P(('gx', 'gy')), may hold values from 0 to 127
- recv_offset: int32 [16384], P(('gx', 'gy')), may hold values from 0 to 511
- weights: float32 [3, 8, 16384], P(None, None, ('gx', 'gy')), may hold values from -3 to 3
Outputs:
- flow_out: float32 [5, 128, 512, 128], P(None, 'gx', 'gy')
- near_out: float32 [5, 16384], P(None, ('gx', 'gy'))
Inputs may be any that keep to these rules, and one draw needn't show every extreme that they name: `donor_owner`: within the fringe points of one device, no owner is named more than 2 times, a bound that some block reaches.
All inputs are finite; a program needn't handle non-finite values.
Results may differ from a plain program's by a relative error of at most 0.0003.
Values sent between devices are 32-bit elements; how exact they have to be, the bound alone decides.
A program may use at most 128 MiB of HBM per device.

v0:
```python
import jax
import jax.numpy as jnp
from jax import lax
from jax.sharding import PartitionSpec as P

STEPS = 2


second_taps = (1.0 / 90, -3.0 / 20, 3.0 / 2, -49.0 / 18, 3.0 / 2, -3.0 / 20, 1.0 / 90)
first_taps = (-1.0 / 60, 3.0 / 20, -3.0 / 4, 0.0, 3.0 / 4, -3.0 / 20, 1.0 / 60)
diffusion = 0.05
velocity = (0.6, -0.5, 0.4)
relaxation = 0.6


def with_halo(block, sides, width):
    for axis, dim in sides:
        count = lax.axis_size(axis)
        forward = [(i, i + 1) for i in range(count - 1)]
        backward = [(target, source) for source, target in forward]
        low = lax.ppermute(
            lax.slice_in_dim(block, block.shape[dim] - width, None, axis=dim), axis, forward
        )
        high = lax.ppermute(lax.slice_in_dim(block, 0, width, axis=dim), axis, backward)
        block = jnp.concatenate([low, block, high], axis=dim)
    return block


def advance(padded, flow):
    extent = flow.shape[1:]
    result = flow
    for axis_pos in range(3):
        total = jnp.zeros_like(flow)
        for offset in range(7):
            factor = diffusion * second_taps[offset] - velocity[axis_pos] * first_taps[offset]
            starts = [3, 3, 3]
            starts[axis_pos] = offset
            piece = padded[
                :,
                starts[0] : starts[0] + extent[0],
                starts[1] : starts[1] + extent[1],
                starts[2] : starts[2] + extent[2],
            ]
            total = total + factor * piece
        result = result + total
    return result


def to_blocks(flow):
    width_v, cells_x, cells_y, cells_z = flow.shape
    shaped = flow.reshape(width_v, cells_x // 8, 8, cells_y // 8, 8, cells_z // 8, 8)
    return jnp.transpose(shaped, (1, 3, 5, 0, 2, 4, 6)).reshape(-1, width_v, 512)


def block_corner(block_ids, cells_y, cells_z):
    blocks_y = cells_y // 8
    blocks_z = cells_z // 8
    first_x = 8 * (block_ids // (blocks_y * blocks_z))
    first_y = 8 * (block_ids // blocks_z % blocks_y)
    first_z = 8 * (block_ids % blocks_z)
    return (first_x, first_y, first_z)


def inject_local(flow, values, block_ids, offsets, live):
    width_v, cells_x, cells_y, cells_z = flow.shape
    first_x, first_y, first_z = block_corner(block_ids, cells_y, cells_z)
    cell_x = first_x + offsets // 64
    cell_y = first_y + offsets // 8 % 8
    cell_z = first_z + offsets % 8
    pick_x = (jnp.arange(cells_x, dtype=jnp.int32)[:, None] == cell_x[None, :]).astype(
        jnp.float32
    ) * live[None, :]
    pick_y = (jnp.arange(cells_y, dtype=jnp.int32)[:, None] == cell_y[None, :]).astype(jnp.float32)
    pick_z = (cell_z[:, None] == jnp.arange(cells_z, dtype=jnp.int32)[None, :]).astype(jnp.float32)
    plane = pick_x[:, None, :] * pick_y[None, :, :]
    left = values.T[:, None, None, :] * plane[None, :, :, :]
    accum = jnp.dot(
        left.reshape(-1, left.shape[-1]), pick_z, precision=lax.Precision.HIGHEST
    ).reshape(flow.shape)
    counts = jnp.dot(
        plane.reshape(-1, plane.shape[-1]), pick_z, precision=lax.Precision.HIGHEST
    ).reshape(cells_x, cells_y, cells_z)
    return (flow + accum) / (1.0 + counts)[None, :, :, :]


def shards(flow, near, donor_owner, donor_block, recv_offset, weights):
    width_v = flow.shape[0]
    fringe_count = near.shape[1]
    devices = lax.axis_size(("gx", "gy"))
    capacity = max(2, 2 * fringe_count // devices)
    slots = devices * capacity
    owner = donor_owner[:, 0]
    onehot = (owner[:, None] == jnp.arange(devices, dtype=jnp.int32)[None, :]).astype(jnp.int32)
    before = jnp.cumsum(onehot, axis=0) - onehot
    rank = jnp.sum(before * onehot, axis=1)
    slot_index = owner * capacity + rank
    for step in range(STEPS):
        padded = with_halo(flow, (("gx", 1), ("gy", 2)), 3)
        padded = jnp.pad(padded, ((0, 0), (0, 0), (0, 0), (3, 3)))
        flow = advance(padded, flow)
        block_table = to_blocks(flow)
        requests = jnp.stack([donor_block, recv_offset, jnp.ones_like(donor_block)], axis=1)
        outgoing = (
            jnp.zeros((slots, 3), jnp.int32)
            .at[slot_index]
            .set(requests)
            .reshape(devices, capacity, 3)
        )
        asked = lax.all_to_all(
            outgoing, ("gx", "gy"), split_axis=0, concat_axis=0, tiled=True
        ).reshape(slots, 3)
        picked = block_table[asked[:, 0]].reshape(devices, capacity, width_v * 512)
        shipped = lax.all_to_all(
            picked, ("gx", "gy"), split_axis=0, concat_axis=0, tiled=True
        ).reshape(slots, width_v, 512)
        mine = shipped[slot_index]
        factor_x = weights[0].T
        factor_y = weights[1].T
        factor_z = weights[2].T
        tensor = (
            factor_x[:, :, None, None] * factor_y[:, None, :, None] * factor_z[:, None, None, :]
        ).reshape(fringe_count, 512)
        interp = jnp.sum(mine * tensor[:, None, :], axis=2).T
        near = near + relaxation * (interp - near)
        sending = (
            jnp.zeros((slots, width_v), jnp.float32)
            .at[slot_index]
            .set(near.T)
            .reshape(devices, capacity, width_v)
        )
        received = lax.all_to_all(
            sending, ("gx", "gy"), split_axis=0, concat_axis=0, tiled=True
        ).reshape(slots, width_v)
        flow = inject_local(
            flow, received, asked[:, 0], asked[:, 1], asked[:, 2].astype(jnp.float32)
        )
    return (flow, near)


def solution(mesh):
    in_specs = (
        P(None, "gx", "gy", None),
        P(None, ("gx", "gy")),
        P(("gx", "gy"), None),
        P(("gx", "gy")),
        P(("gx", "gy")),
        P(None, None, ("gx", "gy")),
    )
    out_specs = (P(None, "gx", "gy", None), P(None, ("gx", "gy")))
    return jax.shard_map(shards, mesh=mesh, in_specs=in_specs, out_specs=out_specs, check_vma=False)
```

profile of v0, /device:TPU:1, one launch (start us, length us, event | category | flops | bytes accessed | tf_op | source)
XLA Modules:
  0.0 322.8 jit_solution(10336271008658861980)
XLA Ops:
  1.7 4.6 %collective-permute-start = (f32[5,3,32,128]{3,2,1,0:T(8,128)S(1)}, f32[5,3,32,128]{3,2,1,0:T(8,128)S(1)}, u32[]{:S(2)}, u32[]{:S(2)}) collective-permute-start(f32[5,3,32,128]{3,2,1,0:T(8,128)S(1)} %get-tuple-element.16), channel_id=1, source_target_pairs={{0,16},{16,32},{32,48},{48,64},{64,80},{80,96},{96,112},{1,17},{17... | collective-permute-start | bytes 737288 | tf_op jit(solution)/shard_map/ppermute | solution.py:21
  9.7 1.5 scatter_custom_fusion
  11.2 9.8 %all-to-all-start = ((s32[128,2,3]{2,1,0:T(2,128)}), s32[128,2,3]{2,1,0:T(2,128)S(1)}, u32[]{:S(2)}, u32[]{:S(2)}) async-start(s32[128,2,3]{2,1,0:T(2,128)} %bitcast.6), calls=%async_computation | async-start | bytes 262144 | tf_op jit(solution)/shard_map/all_to_all | solution.py:109
  21.0 3.0 collective-permute-start.1
  24.0 7.2 %all-to-all-done = s32[128,2,3]{2,1,0:T(2,128)S(1)} async-done(((s32[128,2,3]{2,1,0:T(2,128)}), s32[128,2,3]{2,1,0:T(2,128)S(1)}, u32[]{:S(2)}, u32[]{:S(2)}) %all-to-all-start) | async-done | bytes 3104 | tf_op jit(solution)/shard_map/all_to_all | solution.py:109
  33.0 2.3 collective-permute-start.2
  35.3 1.3 collective-permute-start.3
  37.1 2.6 collective-permute-done.2
  39.7 3.8 %collective-permute-done.3 = f32[5,22,3,128]{3,2,1,0:T(4,128)S(1)} collective-permute-done((f32[5,22,3,128]{3,2,1,0:T(4,128)S(1)}, f32[5,22,3,128]{3,2,1,0:T(4,128)S(1)}, u32[]{:S(2)}, u32[]{:S(2)}) %collective-permute-start.3) | collective-permute-done | bytes 168992 | tf_op jit(solution)/shard_map/ppermute | solution.py:24
  43.5 1.7 select_maximum_fusion.4
  45.2 3.8 %fusion.39 = f32[5,16,32,128]{3,2,1,0:T(8,128)S(1)} fusion(f32[5,22,32,128]{3,2,1,0:T(8,128)S(1)} %get-tuple-element.20, f32[5,22,3,128]{3,2,1,0:T(4,128)S(1)} %collective-permute-done.3, f32[5,22,3,128]{3,2,1,0:T(4,128)S(1)} %collective-permute-done.2, f32[5,22,38,134]{3,2,1,0:T(8,128)S(1)} %select_maximum_fusion.4, f32[5,16,32,128]{3,2,1,0:T(8,128)S(1)} %copy-done, ...), kind=kLoop, calls=%fused_computation.66 | loop fusion | flops 15073280 | bytes 20490240 | tf_op jit(solution)/shard_map/add | solution.py:45
  49.0 13.6 %reshape.271 = f32[5,2,8,4,8,16,8]{6,5,4,3,2,1,0:T(8,128)} reshape(f32[5,16,32,128]{3,2,1,0:T(8,128)S(1)} %fusion.39) | data formatting | bytes 2621440 | tf_op jit(solution)/shard_map/reshape | solution.py:51
  62.6 18.1 %copy.37 = f32[2,4,16,5,8,8,8]{2,1,0,6,5,4,3:T(4,128)} copy(f32[2,4,16,5,8,8,8]{6,2,5,1,4,0,3:T(8,128)} %bitcast.81) | data formatting | bytes 2621440 | tf_op jit(solution)/shard_map/transpose | solution.py:52
  80.7 8.9 %reshape.272 = f32[128,5,512]{0,2,1:T(8,128)S(1)} reshape(f32[2,4,16,5,8,8,8]{2,1,0,6,5,4,3:T(4,128)} %copy.37) | data formatting | bytes 2621440 | tf_op jit(solution)/shard_map/reshape | solution.py:52
  90.7 3.0 gather_fusion
  93.7 5.3 %reshape.275 = f32[128,2,2560]{2,1,0:T(2,128)} reshape(f32[256,5,512]{2,1,0:T(8,128)} %gather_fusion) | data formatting | bytes 5242880 | tf_op jit(solution)/shard_map/reshape | solution.py:112
  99.0 9.3 %all-to-all-start.1 = ((f32[128,2,2560]{2,1,0:T(2,128)}), f32[128,2,2560]{2,1,0:T(2,128)S(1)}, u32[]{:S(2)}, u32[]{:S(2)}) async-start(f32[128,2,2560]{2,1,0:T(2,128)} %reshape.275), calls=%async_computation.1 | async-start | bytes 5242880 | tf_op jit(solution)/shard_map/all_to_all | solution.py:113
  110.3 32.6 %all-to-all-done.1 = f32[128,2,2560]{2,1,0:T(2,128)S(1)} async-done(((f32[128,2,2560]{2,1,0:T(2,128)}), f32[128,2,2560]{2,1,0:T(2,128)S(1)}, u32[]{:S(2)}, u32[]{:S(2)}) %all-to-all-start.1) | async-done | bytes 2621472 | tf_op jit(solution)/shard_map/all_to_all | solution.py:113
  142.9 3.6 %reshape.276 = f32[256,5,512]{2,1,0:T(8,128)} reshape(f32[128,2,2560]{2,1,0:T(2,128)S(1)} %all-to-all-done.1) | data formatting | bytes 5242880 | tf_op jit(solution)/shard_map/reshape | solution.py:115
  146.5 2.9 gather_fusion.1
  149.4 1.4 multiply_reduce_fusion.1
  150.8 1.6 scatter_custom_fusion.1
  152.4 5.3 %all-to-all-start.2 = ((f32[128,2,5]{2,1,0:T(2,128)}), f32[128,2,5]{2,1,0:T(2,128)S(1)}, u32[]{:S(2)}, u32[]{:S(2)}) async-start(f32[128,2,5]{2,1,0:T(2,128)} %bitcast.18), calls=%async_computation.2 | async-start | bytes 262144 | tf_op jit(solution)/shard_map/all_to_all | solution.py:131
  157.7 1.2 convolution_add_fusion
  159.0 9.0 %all-to-all-done.2 = f32[128,2,5]{2,1,0:T(2,128)S(1)} async-done(((f32[128,2,5]{2,1,0:T(2,128)}), f32[128,2,5]{2,1,0:T(2,128)S(1)}, u32[]{:S(2)}, u32[]{:S(2)}) %all-to-all-start.2) | async-done | bytes 5152 | tf_op jit(solution)/shard_map/all_to_all | solution.py:131
  168.0 2.5 fusion.8
  170.5 2.6 collective-permute-start.4
  173.1 1.9 collective-permute-start.5
  176.2 4.4 %collective-permute-done.5 = f32[5,3,32,128]{3,2,1,0:T(8,128)S(1)} collective-permute-done((f32[5,3,32,128]{3,2,1,0:T(8,128)S(1)}, f32[5,3,32,128]{3,2,1,0:T(8,128)S(1)}, u32[]{:S(2)}, u32[]{:S(2)}) %collective-permute-start.5) | collective-permute-done | bytes 245792 | tf_op jit(solution)/shard_map/ppermute | solution.py:24
  180.7 2.3 collective-permute-start.6
  183.0 1.3 collective-permute-start.7
  184.3 1.6 collective-permute-done.6
  185.9 3.8 %collective-permute-done.7 = f32[5,22,3,128]{3,2,1,0:T(4,128)S(1)} collective-permute-done((f32[5,22,3,128]{3,2,1,0:T(4,128)S(1)}, f32[5,22,3,128]{3,2,1,0:T(4,128)S(1)}, u32[]{:S(2)}, u32[]{:S(2)}) %collective-permute-start.7) | collective-permute-done | bytes 168992 | tf_op jit(solution)/shard_map/ppermute | solution.py:24
  189.7 4.1 %select_maximum_fusion = f32[5,22,38,134]{3,2,1,0:T(8,128)S(1)} fusion(f32[5,22,3,128]{3,2,1,0:T(4,128)S(1)} %collective-permute-done.7, f32[5,22,3,128]{3,2,1,0:T(4,128)S(1)} %collective-permute-done.6, f32[5,3,32,128]{3,2,1,0:T(8,128)S(1)} %collective-permute-done.5, f32[5,16,32,128]{3,2,1,0:T(8,128)S(1)} %fusion.8, ...), kind=kLoop, calls=%fused_computation.9 | loop fusion | flops 6721440 | bytes 4380640 | tf_op jit(solution)/shard_map/concatenate | solution.py:25
  194.2 3.9 %fusion.23 = f32[5,16,32,128]{3,2,1,0:T(8,128)S(1)} fusion(f32[5,16,32,128]{3,2,1,0:T(8,128)S(1)} %fusion.8, f32[5,3,32,128]{3,2,1,0:T(8,128)S(1)} %collective-permute-done.5, f32[5,3,32,128]{3,2,1,0:T(8,128)S(1)} %collective-permute-done.4, f32[5,22,38,134]{3,2,1,0:T(8,128)S(1)} %select_maximum_fusion, f32[5,22,35,128]{3,2,1,0:T(8,128)S(1)} %get-tuple-element.5, ...), kind=kLoop, calls=%fused_computation.50 | loop fusion | flops 15073280 | bytes 18841600 | tf_op jit(solution)/shard_map/add | solution.py:45
  198.1 13.6 %reshape.279 = f32[5,2,8,4,8,16,8]{6,5,4,3,2,1,0:T(8,128)} reshape(f32[5,16,32,128]{3,2,1,0:T(8,128)S(1)} %fusion.23) | data formatting | bytes 2621440 | tf_op jit(solution)/shard_map/reshape | solution.py:51
  211.7 18.1 %copy.45 = f32[2,4,16,5,8,8,8]{2,1,0,6,5,4,3:T(4,128)} copy(f32[2,4,16,5,8,8,8]{6,2,5,1,4,0,3:T(8,128)} %bitcast.82) | data formatting | bytes 2621440 | tf_op jit(solution)/shard_map/transpose | solution.py:52
  229.7 8.9 %reshape.280 = f32[128,5,512]{0,2,1:T(8,128)S(1)} reshape(f32[2,4,16,5,8,8,8]{2,1,0,6,5,4,3:T(4,128)} %copy.45) | data formatting | bytes 2621440 | tf_op jit(solution)/shard_map/reshape | solution.py:52
  239.8 3.1 gather_fusion.2
  242.9 4.2 %reshape.281 = f32[128,2,2560]{2,1,0:T(2,128)S(1)} reshape(f32[256,5,512]{2,1,0:T(8,128)} %gather_fusion.2) | data formatting | bytes 5242880 | tf_op jit(solution)/shard_map/reshape | solution.py:112
  247.2 45.0 %all_to_all.26 = f32[128,2,2560]{2,1,0:T(2,128)} all-to-all(f32[128,2,2560]{2,1,0:T(2,128)S(1)} %reshape.281), channel_id=1, replica_groups=mesh['gx'=8,'gy'=16] {'gx','gy'}, dimensions={0} | all-to-all | bytes 5242880 | tf_op jit(solution)/shard_map/all_to_all | solution.py:113
  292.2 5.3 %reshape.282 = f32[256,5,512]{2,1,0:T(8,128)} reshape(f32[128,2,2560]{2,1,0:T(2,128)} %all_to_all.26) | data formatting | bytes 5242880 | tf_op jit(solution)/shard_map/reshape | solution.py:115
  297.5 3.0 gather_fusion.3
  300.5 1.4 multiply_reduce_fusion
  302.0 1.6 scatter_custom_fusion.2
  303.6 5.3 %all-to-all-start.4 = ((f32[128,2,5]{2,1,0:T(2,128)}), f32[128,2,5]{2,1,0:T(2,128)S(1)}, u32[]{:S(2)}, u32[]{:S(2)}) async-start(f32[128,2,5]{2,1,0:T(2,128)} %bitcast.31), calls=%async_computation.4 | async-start | bytes 262144 | tf_op jit(solution)/shard_map/all_to_all | solution.py:131
  309.6 9.5 %all-to-all-done.4 = f32[128,2,5]{2,1,0:T(2,128)S(1)} async-done(((f32[128,2,5]{2,1,0:T(2,128)}), f32[128,2,5]{2,1,0:T(2,128)S(1)}, u32[]{:S(2)}, u32[]{:S(2)}) %all-to-all-start.4) | async-done | bytes 5152 | tf_op jit(solution)/shard_map/all_to_all | solution.py:131
  319.2 3.6 %fusion.14 = f32[5,16,32,128]{3,2,1,0:T(8,128)} fusion(f32[5,16,32,128]{3,2,1,0:T(8,128)S(1)} %copy-done.2, f32[5,256]{1,0:T(8,128)S(1)} %bitcast.89, f32[16,32,256]{2,1,0:T(8,128)} %broadcast_multiply_fusion, f32[16,32,128]{2,1,0:T(8,128)} %copy-done.7, s32[256]{0:T(256)S(1)} %bitcast.94), kind=kOutput, calls=%fused_computation.43 | convolution fusion | flops 1007976448 | bytes 3414016 | tf_op jit(solution)/shard_map/dot_general | solution.py:77
  (68 shorter events, 13.5 us)
Async XLA Ops:
  1.7 30.5 %copy-start = (f32[5,16,32,128]{3,2,1,0:T(8,128)S(1)}, f32[5,16,32,128]{3,2,1,0:T(8,128)}, u32[]{:S(2)}) copy-start(f32[5,16,32,128]{3,2,1,0:T(8,128)} %param.6) | copy-start | bytes 3932164
  1.7 30.5 %collective-permute-start = (f32[5,3,32,128]{3,2,1,0:T(8,128)S(1)}, f32[5,3,32,128]{3,2,1,0:T(8,128)S(1)}, u32[]{:S(2)}, u32[]{:S(2)}) collective-permute-start(f32[5,3,32,128]{3,2,1,0:T(8,128)S(1)} %get-tuple-element.16), channel_id=1, source_target_pairs={{0,16},{16,32},{32,48},{48,64},{64,80},{80,96},{96,112},{1,17},{17... | collective-permute-start | bytes 737288 | tf_op jit(solution)/shard_map/ppermute | solution.py:21
  9.6 99.7 %copy-start.13 = (s32[128]{0:T(128)}, s32[128]{0:T(128)S(1)}, u32[]{:S(2)}) copy-start(s32[128]{0:T(128)S(1)} %fusion.115) | copy-start | bytes 1540
  11.2 20.0 %all-to-all-start = ((s32[128,2,3]{2,1,0:T(2,128)}), s32[128,2,3]{2,1,0:T(2,128)S(1)}, u32[]{:S(2)}, u32[]{:S(2)}) async-start(s32[128,2,3]{2,1,0:T(2,128)} %bitcast.6), calls=%async_computation | async-start | bytes 262144 | tf_op jit(solution)/shard_map/all_to_all | solution.py:109
  21.0 11.8 %collective-permute-start.1 = (f32[5,3,32,128]{3,2,1,0:T(8,128)S(1)}, f32[5,3,32,128]{3,2,1,0:T(8,128)S(1)}, u32[]{:S(2)}, u32[]{:S(2)}) collective-permute-start(f32[5,3,32,128]{3,2,1,0:T(8,128)S(1)} %get-tuple-element.15), channel_id=1, source_target_pairs={{16,0},{32,16},{48,32},{64,48},{80,64},{96,80},{112,96},{17,1},{33... | collective-permute-start | bytes 737288 | tf_op jit(solution)/shard_map/ppermute | solution.py:24
  33.0 6.7 %collective-permute-start.2 = (f32[5,22,3,128]{3,2,1,0:T(4,128)S(1)}, f32[5,22,3,128]{3,2,1,0:T(4,128)S(1)}, u32[]{:S(2)}, u32[]{:S(2)}) collective-permute-start(f32[5,22,3,128]{3,2,1,0:T(4,128)S(1)} %get-tuple-element.8), channel_id=1, source_target_pairs={{0,1},{1,2},{2,3},{3,4},{4,5},{5,6},{6,7},{7,8},{8,9},{9,10},{10,1... | collective-permute-start | bytes 506888 | tf_op jit(solution)/shard_map/ppermute | solution.py:21
  35.3 8.2 %collective-permute-start.3 = (f32[5,22,3,128]{3,2,1,0:T(4,128)S(1)}, f32[5,22,3,128]{3,2,1,0:T(4,128)S(1)}, u32[]{:S(2)}, u32[]{:S(2)}) collective-permute-start(f32[5,22,3,128]{3,2,1,0:T(4,128)S(1)} %get-tuple-element.9), channel_id=1, source_target_pairs={{1,0},{2,1},{3,2},{4,3},{5,4},{6,5},{7,6},{8,7},{9,8},{10,9},{11,1... | collective-permute-start | bytes 506888 | tf_op jit(solution)/shard_map/ppermute | solution.py:24
  37.1 53.6 %copy-start.9 = (s32[1024]{0:T(1024)}, s32[1024]{0:T(1024)S(1)}, u32[]{:S(2)}) copy-start(s32[1024]{0:T(1024)S(1)} %pad_clamp_fusion.1) | copy-start | bytes 12292
  49.0 13.6 %copy-start.3 = (f32[5,16,32,128]{3,2,1,0:T(8,128)}, f32[5,16,32,128]{3,2,1,0:T(8,128)S(1)}, u32[]{:S(2)}) copy-start(f32[5,16,32,128]{3,2,1,0:T(8,128)S(1)} %fusion.39) | copy-start | bytes 3932164
  99.0 9.3 %copy-start.12 = (f32[5,128]{1,0:T(8,128)S(1)}, f32[5,128]{1,0:T(8,128)}, u32[]{:S(2)}) copy-start(f32[5,128]{1,0:T(8,128)} %param.7) | copy-start | bytes 7684
  99.0 9.4 %copy-start.8 = (f32[3,8,128]{2,1,0:T(8,128)S(1)}, f32[3,8,128]{2,1,0:T(8,128)}, u32[]{:S(2)}) copy-start(f32[3,8,128]{2,1,0:T(8,128)} %param.11) | copy-start | bytes 36868
  99.0 10.3 %copy-start.5 = (f32[256,1]{1,0:T(8,128)S(1)}, f32[256,1]{1,0:T(8,128)}, u32[]{:S(2)}) copy-start(f32[256,1]{1,0:T(8,128)} %get-tuple-element.21) | copy-start | bytes 3076
  99.0 43.9 %all-to-all-start.1 = ((f32[128,2,2560]{2,1,0:T(2,128)}), f32[128,2,2560]{2,1,0:T(2,128)S(1)}, u32[]{:S(2)}, u32[]{:S(2)}) async-start(f32[128,2,2560]{2,1,0:T(2,128)} %reshape.275), calls=%async_computation.1 | async-start | bytes 5242880 | tf_op jit(solution)/shard_map/all_to_all | solution.py:113
  109.3 37.2 %copy-start.10 = (s32[1024]{0:T(1024)}, s32[1024]{0:T(1024)S(1)}, u32[]{:S(2)}) copy-start(s32[1024]{0:T(1024)S(1)} %pad_clamp_fusion) | copy-start | bytes 12292
  109.5 37.0 %copy-start.6 = (f32[32,256]{1,0:T(8,128)}, f32[32,256]{1,0:T(8,128)S(1)}, u32[]{:S(2)}) copy-start(f32[32,256]{1,0:T(8,128)S(1)} %fusion.103) | copy-start | bytes 98308
  149.4 18.6 %copy-start.4 = (f32[5,16,32,128]{3,2,1,0:T(8,128)S(1)}, f32[5,16,32,128]{3,2,1,0:T(8,128)}, u32[]{:S(2)}) copy-start(f32[5,16,32,128]{3,2,1,0:T(8,128)} %copy-done.3) | copy-start | bytes 3932164
  152.4 15.5 %all-to-all-start.2 = ((f32[128,2,5]{2,1,0:T(2,128)}), f32[128,2,5]{2,1,0:T(2,128)S(1)}, u32[]{:S(2)}, u32[]{:S(2)}) async-start(f32[128,2,5]{2,1,0:T(2,128)} %bitcast.18), calls=%async_computation.2 | async-start | bytes 262144 | tf_op jit(solution)/shard_map/all_to_all | solution.py:131
  158.9 11.6 %copy-start.7 = (f32[16,32,128]{2,1,0:T(8,128)}, f32[16,32,128]{2,1,0:T(8,128)S(1)}, u32[]{:S(2)}) copy-start(f32[16,32,128]{2,1,0:T(8,128)S(1)} %convolution_add_fusion) | copy-start | bytes 786436
  170.5 5.7 %collective-permute-start.4 = (f32[5,3,32,128]{3,2,1,0:T(8,128)S(1)}, f32[5,3,32,128]{3,2,1,0:T(8,128)S(1)}, u32[]{:S(2)}, u32[]{:S(2)}) collective-permute-start(f32[5,3,32,128]{3,2,1,0:T(8,128)S(1)} %get-tuple-element.10), channel_id=1, source_target_pairs={{0,16},{16,32},{32,48},{48,64},{64,80},{80,96},{96,112},{1,17},{17... | collective-permute-start | bytes 737288 | tf_op jit(solution)/shard_map/ppermute | solution.py:21
  173.1 7.5 %collective-permute-start.5 = (f32[5,3,32,128]{3,2,1,0:T(8,128)S(1)}, f32[5,3,32,128]{3,2,1,0:T(8,128)S(1)}, u32[]{:S(2)}, u32[]{:S(2)}) collective-permute-start(f32[5,3,32,128]{3,2,1,0:T(8,128)S(1)} %get-tuple-element.11), channel_id=1, source_target_pairs={{16,0},{32,16},{48,32},{64,48},{80,64},{96,80},{112,96},{17,1},{33... | collective-permute-start | bytes 737288 | tf_op jit(solution)/shard_map/ppermute | solution.py:24
  180.7 5.2 %collective-permute-start.6 = (f32[5,22,3,128]{3,2,1,0:T(4,128)S(1)}, f32[5,22,3,128]{3,2,1,0:T(4,128)S(1)}, u32[]{:S(2)}, u32[]{:S(2)}) collective-permute-start(f32[5,22,3,128]{3,2,1,0:T(4,128)S(1)} %get-tuple-element.6), channel_id=1, source_target_pairs={{0,1},{1,2},{2,3},{3,4},{4,5},{5,6},{6,7},{7,8},{8,9},{9,10},{10,1... | collective-permute-start | bytes 506888 | tf_op jit(solution)/shard_map/ppermute | solution.py:21
  183.0 6.7 %collective-permute-start.7 = (f32[5,22,3,128]{3,2,1,0:T(4,128)S(1)}, f32[5,22,3,128]{3,2,1,0:T(4,128)S(1)}, u32[]{:S(2)}, u32[]{:S(2)}) collective-permute-start(f32[5,22,3,128]{3,2,1,0:T(4,128)S(1)} %get-tuple-element.7), channel_id=1, source_target_pairs={{1,0},{2,1},{3,2},{4,3},{5,4},{6,5},{7,6},{8,7},{9,8},{10,9},{11,1... | collective-permute-start | bytes 506888 | tf_op jit(solution)/shard_map/ppermute | solution.py:24
  198.1 13.6 %copy-start.1 = (f32[5,16,32,128]{3,2,1,0:T(8,128)}, f32[5,16,32,128]{3,2,1,0:T(8,128)S(1)}, u32[]{:S(2)}) copy-start(f32[5,16,32,128]{3,2,1,0:T(8,128)S(1)} %fusion.23) | copy-start | bytes 3932164
  300.5 18.7 %copy-start.2 = (f32[5,16,32,128]{3,2,1,0:T(8,128)S(1)}, f32[5,16,32,128]{3,2,1,0:T(8,128)}, u32[]{:S(2)}) copy-start(f32[5,16,32,128]{3,2,1,0:T(8,128)} %copy-done.1) | copy-start | bytes 3932164
  300.5 18.7 %copy-start.11 = (s32[256,1]{0,1:T(1,128)S(1)}, s32[256,1]{0,1:T(1,128)}, u32[]{:S(2)}) copy-start(s32[256,1]{0,1:T(1,128)} %get-tuple-element.29) | copy-start | bytes 3076
  303.6 15.5 %all-to-all-start.4 = ((f32[128,2,5]{2,1,0:T(2,128)}), f32[128,2,5]{2,1,0:T(2,128)S(1)}, u32[]{:S(2)}, u32[]{:S(2)}) async-start(f32[128,2,5]{2,1,0:T(2,128)} %bitcast.31), calls=%async_computation.4 | async-start | bytes 262144 | tf_op jit(solution)/shard_map/all_to_all | solution.py:131
where the time goes:
time: 325 us; the launch traced here: 323 us
  local copies, waits for them, and re-layouts  121 us (37%)
  waiting for transfers between devices  75.7 us (23%)
  starting transfers between devices  49 us (15%)
  blocking collectives  45 us (14%)
  other arithmetic  23.8 us (7%)
  matrix products  7.29 us (2%)
    all_to_all x1, blocking collectives, shards(): lax.all_to_all(picked, ('gx', 'gy'), split_axis=0, concat_axis=0, tiled=T...  45 us
    transpose x2, local copies, waits for them, and re-layouts, to_blocks(): jnp.transpose(shaped, (1, 3, 5, 0, 2, 4, 6)).reshape(-1, width_v, 512)  36.1 us
    all_to_all x1, waiting for transfers between devices, shards(): lax.all_to_all(picked, ('gx', 'gy'), split_axis=0, concat_axis=0, tiled=T...  32.6 us
    reshape x2, local copies, waits for them, and re-layouts, to_blocks(): flow.reshape(width_v, cells_x // 8, 8, cells_y // 8, 8, cells_z // 8, 8)  27.1 us
    reshape x4, local copies, waits for them, and re-layouts, to_blocks(): jnp.transpose(shaped, (1, 3, 5, 0, 2, 4, 6)).reshape(-1, width_v, 512)  20.1 us
    all_to_all x2, waiting for transfers between devices, shards(): lax.all_to_all(sending, ('gx', 'gy'), split_axis=0, concat_axis=0, tiled=...  18.5 us
    ppermute x4, waiting for transfers between devices, with_halo(): lax.ppermute(lax.slice_in_dim(block, 0, width, axis=dim), axis, backward)  12 us
    ppermute x4, starting transfers between devices, with_halo(): lax.ppermute(lax.slice_in_dim(block, block.shape[dim] - width, None, axis...  11.7 us
  transfers between devices with their start and end apart: 12, of which 10 were waited for; matrix products, arithmetic and copies ran while one was open for 3% of the time, Pallas kernels for 0%

commit v1 on v0

v1 whole, which is shorter than its diff:
```python
import functools

import jax
import jax.numpy as jnp
from jax import lax
from jax.experimental import pallas as pl
from jax.experimental.pallas import tpu as pltpu
from jax.sharding import PartitionSpec as P

STEPS = 2
NV = 5
CX = 16
CY = 32
CZ = 128
FR = 128
GX = 8
GY = 16
DEVICES = GX * GY
SLOTS = 2 * DEVICES
PX = CX + 6
PY = CY + 16
Y0 = 8

second_taps = (1.0 / 90, -3.0 / 20, 3.0 / 2, -49.0 / 18, 3.0 / 2, -3.0 / 20, 1.0 / 90)
first_taps = (-1.0 / 60, 3.0 / 20, -3.0 / 4, 0.0, 3.0 / 4, -3.0 / 20, 1.0 / 60)
diffusion = 0.05
velocity = (0.6, -0.5, 0.4)
relaxation = 0.6

TAPS = [
    [diffusion * second_taps[o] - velocity[d] * first_taps[o] for o in range(7)] for d in range(3)
]
CENTER = 1.0 + sum(TAPS[d][3] for d in range(3))
OFFSETS = (-3, -2, -1, 1, 2, 3)
HIGHEST = lax.Precision.HIGHEST
MESH = pl.DeviceIdType.MESH
BF16 = jnp.bfloat16
F32 = jnp.float32


def tap(dim, j):
    return TAPS[dim][j + 3]


def split(value):
    high = value.astype(BF16)
    low = (value - high.astype(F32)).astype(BF16)
    return high, low


def kernel(
    flow_hbm, near_hbm, owner_hbm, block_hbm, offset_hbm, weights_hbm,
    flow_out, near_out,
    g0, g1, res, hx, hy, sy,
    near_in, owner_in, block_in, offset_in, weights_in, near_res,
    a1, b1, bt, c1, d1, e1, et, fin,
    ohot, wz_rhs, plane, pick, pzt, recip,
    in_sem, small_sem, halo_send, halo_recv, a2a_send, a2a_recv, out_sem, near_sem,
):
    gx = lax.axis_index("gx")
    gy = lax.axis_index("gy")

    small = [
        pltpu.make_async_copy(src, dst, small_sem.at[i])
        for i, (src, dst) in enumerate(
            (
                (owner_hbm, owner_in),
                (block_hbm, block_in),
                (offset_hbm, offset_in),
                (near_hbm, near_in),
                (weights_hbm, weights_in),
            )
        )
    ]
    for copy in small:
        copy.start()

    def flow_in(v):
        return pltpu.make_async_copy(
            flow_hbm.at[v],
            g0.at[pl.ds(v * PX + 3, CX), pl.ds(Y0, CY)],
            in_sem.at[v],
        )

    for v in range(NV):
        flow_in(v).start()

    hx[...] = jnp.zeros_like(hx)
    hy[...] = jnp.zeros_like(hy)

    barrier = pltpu.get_barrier_semaphore()
    for k in range(1, GX):
        pl.semaphore_signal(
            barrier, inc=1, device_id=(lax.rem(gx + k, GX), gy), device_id_type=MESH
        )
    for k in range(1, GY):
        pl.semaphore_signal(
            barrier, inc=1, device_id=(gx, lax.rem(gy + k, GY)), device_id_type=MESH
        )

    def clear(v, carry):
        for g in (g0, g1):
            for x in (0, 1, 2, PX - 3, PX - 2, PX - 1):
                g[v * PX + x, Y0 : Y0 + CY] = jnp.zeros((CY, CZ), F32)
            for x in range(3, PX - 3):
                g[v * PX + x, 0:Y0] = jnp.zeros((Y0, CZ), F32)
                g[v * PX + x, Y0 + CY : PY] = jnp.zeros((PY - Y0 - CY, CZ), F32)
        return carry

    lax.fori_loop(0, NV, clear, 0)

    for copy in small:
        copy.wait()
    owner_row = owner_in[...]
    row = lax.broadcasted_iota(jnp.int32, (FR, FR), 0)
    col = lax.broadcasted_iota(jnp.int32, (FR, FR), 1)
    owner_wide = jnp.broadcast_to(owner_row, (FR, FR))
    owner_tall = jnp.transpose(owner_wide)
    earlier = jnp.where((owner_wide == owner_tall) & (row < col), 1.0, 0.0).astype(F32)
    rank = jnp.sum(earlier, axis=0, keepdims=True)
    mine = owner_wide == row
    ohot[0] = jnp.where(mine & (rank < 0.5), 1.0, 0.0).astype(F32)
    ohot[1] = jnp.where(mine & (rank > 0.5), 1.0, 0.0).astype(F32)
    payload = jnp.concatenate(
        [
            weights_in[...],
            near_in[...],
            block_in[...].astype(F32),
            offset_in[...].astype(F32),
            jnp.ones((1, FR), F32),
        ],
        axis=0,
    )
    nothing = jnp.zeros((32, FR), F32)
    blank = jnp.zeros((64, FR), F32)
    contract_last = (((1,), (1,)), ((), ()))
    rows = lax.dot_general(
        ohot[0], jnp.concatenate([payload, nothing, blank], axis=0), contract_last,
        precision=HIGHEST, preferred_element_type=F32,
    ) + lax.dot_general(
        ohot[1], jnp.concatenate([nothing, payload, blank], axis=0), contract_last,
        precision=HIGHEST, preferred_element_type=F32,
    )
    a1[...] = rows.reshape(GX, GY, 128)

    pl.semaphore_wait(barrier, GX - 1 + GY - 1)

    def exchange_x(src, dst, phase):
        def send(k, carry):
            peer = lax.rem(gx + k, GX)
            pltpu.make_async_remote_copy(
                src_ref=src.at[peer], dst_ref=dst.at[gx],
                send_sem=a2a_send.at[phase], recv_sem=a2a_recv.at[phase],
                device_id=(peer, gy), device_id_type=MESH,
            ).start()
            return carry

        lax.fori_loop(1, GX, send, 0)
        dst[gx] = src[gx]

    def exchange_y(src, dst, phase):
        def send(k, carry):
            peer = lax.rem(gy + k, GY)
            pltpu.make_async_remote_copy(
                src_ref=src.at[peer], dst_ref=dst.at[gy],
                send_sem=a2a_send.at[phase], recv_sem=a2a_recv.at[phase],
                device_id=(gx, peer), device_id_type=MESH,
            ).start()
            return carry

        lax.fori_loop(1, GY, send, 0)
        dst[gy] = src[gy]

    def exchange_wait(buf, count, sem):
        part = buf.at[pl.ds(0, count - 1)]
        pltpu.make_async_copy(part, part, sem).wait()

    exchange_x(a1, b1, 0)

    def face(step, v, side):
        g = (g0, g1)[step]
        if side < 2:
            first = 3 + (CX - 3 if side == 0 else 0)
            src = g.at[pl.ds(v * PX + first, 3), pl.ds(Y0, CY)]
            dst = hx.at[step, v, side]
            target = (gx + (1 if side == 0 else -1), gy)
        else:
            src = sy.at[step, v, side - 2]
            dst = hy.at[step, v, side - 2]
            target = (gx, gy + (1 if side == 2 else -1))
        return pltpu.make_async_remote_copy(
            src_ref=src, dst_ref=dst,
            send_sem=halo_send.at[step, v, side], recv_sem=halo_recv.at[step, v, side],
            device_id=target, device_id_type=MESH,
        )

    sends = (gx < GX - 1, gx > 0, gy < GY - 1, gy > 0)
    takes = (gx > 0, gx < GX - 1, gy > 0, gy < GY - 1)

    def send_faces(step, v):
        flat = (g0, g1)[step].reshape(NV * PX * PY, CZ)
        for side in (0, 1):
            @pl.when(sends[side])
            def _():
                face(step, v, side).start()
        for side, first in ((0, CY - 3), (1, 0)):
            for j in range(3):
                for half in range(2):
                    start = (v * PX + 3 + 8 * half) * PY + Y0 + first + j
                    sy[step, v, side, pl.ds(j * CX + 8 * half, 8)] = flat[pl.ds(start, 8, PY)]
        for side in (2, 3):
            @pl.when(sends[side])
            def _():
                face(step, v, side).start()

    def first_faces(v, carry):
        flow_in(v).wait()
        send_faces(0, v)
        return carry

    lax.fori_loop(0, NV, first_faces, 0)

    lane = lax.broadcasted_iota(jnp.int32, (8, CZ), 1)
    along_z = [
        jnp.where((lane + j >= 0) & (lane + j < CZ), tap(2, j), 0.0).astype(F32) for j in OFFSETS
    ]

    def interior(step, low, high):
        g = (g0, g1)[step]

        def body(i, carry):
            at = (i // CX) * PX + lax.rem(i, CX) + 3
            mid = g[at, Y0 : Y0 + CY]
            total = mid * CENTER
            for j in OFFSETS:
                total = total + g[at + j, Y0 : Y0 + CY] * tap(0, j)
            for j in OFFSETS:
                total = total + g[at, Y0 + j : Y0 + CY + j] * tap(1, j)
            tiles = mid.reshape(CY // 8, 8, CZ)
            for k, j in enumerate(OFFSETS):
                moved = pltpu.roll(mid, (-j) % CZ, axis=1).reshape(CY // 8, 8, CZ)
                total = total + (moved * along_z[k][None]).reshape(CY, CZ)
            res[i] = total
            return carry

        lax.fori_loop(low * CX, high * CX, body, 0)

    interior(0, 0, 2)

    exchange_wait(b1, GX, a2a_recv.at[0])
    b_flat = b1.reshape(GX * GY, 128)
    for h in range(GY):
        bt[h] = b_flat[pl.ds(h, GX, GY)]
    exchange_y(bt, c1, 1)

    interior(0, 2, NV)

    exchange_wait(c1, GY, a2a_recv.at[1])
    table = jnp.transpose(c1[...].reshape(DEVICES, 128))
    asked = jnp.concatenate([table[0:32], table[32:64]], axis=1)
    wx = asked[0:8]
    wy = asked[8:16]
    wz = asked[16:24]
    last = asked[24:32]
    block = last[5:6].astype(jnp.int32)
    offset = last[6:7].astype(jnp.int32)
    live = last[7:8]
    row8 = lax.broadcasted_iota(jnp.int32, (8, SLOTS), 0)
    near = jnp.where(row8 < NV, last, 0.0)
    kx = block // 64
    ky = (block // 16) % 4
    kz = block % 16
    weights_z = jnp.concatenate(
        [jnp.where(kz == b, wz, 0.0) for b in range(CZ // 8)], axis=0
    )
    z_high, z_low = split(weights_z)
    wz_rhs[0:CZ] = z_high
    wz_rhs[CZ : 2 * CZ] = z_high
    wz_rhs[2 * CZ :] = z_low
    weights_x = jnp.concatenate([jnp.where(kx == b, wx, 0.0) for b in range(CX // 8)], axis=0)
    weights_y = jnp.concatenate([jnp.where(ky == b, wy, 0.0) for b in range(CY // 8)], axis=0)
    for x in range(CX):
        plane[x * CY : (x + 1) * CY] = weights_x[x : x + 1] * weights_y
    cell = (8 * kx + offset // 64) * CY + 8 * ky + (offset // 8) % 8
    cell = jnp.where(live > 0.5, cell, -1)
    cell_z = 8 * kz + offset % 8
    places = lax.broadcasted_iota(jnp.int32, (CX * CY, SLOTS), 0)
    pick[...] = jnp.where(places == cell, 1.0, 0.0).astype(F32).astype(BF16)
    places_z = lax.broadcasted_iota(jnp.int32, (CZ, SLOTS), 0)
    hot_z = jnp.where(places_z == cell_z, 1.0, 0.0).astype(F32).astype(BF16)
    pzt[:, 0:SLOTS] = hot_z
    pzt[:, SLOTS:] = hot_z
    counts = lax.dot_general(
        pick[...], hot_z, contract_last, preferred_element_type=F32
    )
    recip[...] = 1.0 / (1.0 + counts)

    flat_res = res.reshape(NV * CX * CY, CZ)

    def add_halo(step, v):
        for r in range(3):
            low = res[v * CX + r]
            high = res[v * CX + CX - 1 - r]
            for j in range(-3, -r):
                low = low + hx[step, v, 0, r + j + 3] * tap(0, j)
                high = high + hx[step, v, 1, -r - 1 - j] * tap(0, -j)
            res[v * CX + r] = low
            res[v * CX + CX - 1 - r] = high
        for r in range(3):
            for half in range(2):
                start = (v * CX + 8 * half) * CY
                at_low = pl.ds(start + r, 8, CY)
                at_high = pl.ds(start + CY - 1 - r, 8, CY)
                low = flat_res[at_low]
                high = flat_res[at_high]
                for j in range(-3, -r):
                    low = low + hy[step, v, 0, pl.ds((r + j + 3) * CX + 8 * half, 8)] * tap(1, j)
                    high = high + hy[step, v, 1, pl.ds((-r - 1 - j) * CX + 8 * half, 8)] * tap(1, -j)
                flat_res[at_low] = low
                flat_res[at_high] = high

    def finish_flow(step, near):
        def body(v, interp):
            for side in range(4):
                @pl.when(takes[side])
                def _():
                    face(step, v, side).wait_recv()
            add_halo(step, v)
            values = flat_res[pl.ds(pl.multiple_of(v * CX * CY, CX * CY), CX * CY)]
            high, low = split(values)
            t = jnp.dot(
                jnp.concatenate([high, low, high], axis=1), wz_rhs[...],
                preferred_element_type=F32,
            )
            here = jnp.sum(t * plane[...], axis=0, keepdims=True)
            return jnp.where(row8 == v, here, interp)

        interp = lax.fori_loop(0, NV, body, jnp.zeros((8, SLOTS), F32))
        return near + relaxation * (interp - near)

    def injected(v, near):
        here = jnp.sum(jnp.where(row8 == v, near, 0.0), axis=0, keepdims=True)
        here = jnp.broadcast_to(here, (16, SLOTS))
        high, low = split(here)
        hot = pick[...].reshape(CX * CY // 16, 16, SLOTS)
        left = jnp.concatenate(
            [
                (hot * high[None]).reshape(CX * CY, SLOTS),
                (hot * low[None]).reshape(CX * CY, SLOTS),
            ],
            axis=1,
        )
        gained = lax.dot_general(left, pzt[...], contract_last, preferred_element_type=F32)
        values = flat_res[pl.ds(pl.multiple_of(v * CX * CY, CX * CY), CX * CY)]
        return ((values + gained) * recip[...]).reshape(CX, CY, CZ)

    near = finish_flow(0, near)

    def second_faces(v, carry):
        g1[pl.ds(v * PX + 3, CX), Y0 : Y0 + CY] = injected(v, near)
        send_faces(1, v)
        return carry

    lax.fori_loop(0, NV, second_faces, 0)
    interior(1, 0, NV)
    near = finish_flow(1, near)

    back = jnp.concatenate(
        [near[:, :DEVICES], near[:, DEVICES:], jnp.zeros((DEVICES - 16, DEVICES), F32)], axis=0
    )
    d1[...] = jnp.transpose(back).reshape(GY, GX, 128)
    exchange_y(d1, e1, 2)

    def flow_back(v):
        return pltpu.make_async_copy(
            res.at[pl.ds(v * CX, CX)], flow_out.at[v], out_sem.at[v]
        )

    def last_injection(v, carry):
        res[pl.ds(v * CX, CX)] = injected(v, near)
        flow_back(v).start()
        return carry

    lax.fori_loop(0, 3, last_injection, 0)
    exchange_wait(e1, GY, a2a_recv.at[2])
    e_flat = e1.reshape(GX * GY, 128)
    for g in range(GX):
        for half in range(2):
            et[g, 8 * half : 8 * half + 8] = e_flat[pl.ds(8 * half * GX + g, 8, GX)]
    exchange_x(et, fin, 3)
    lax.fori_loop(3, NV, last_injection, 0)
    exchange_wait(fin, GX, a2a_recv.at[3])
    returned = jnp.transpose(fin[...].reshape(DEVICES, 128))
    served = jnp.dot(
        returned[0:8], ohot[0], precision=HIGHEST, preferred_element_type=F32
    ) + jnp.dot(returned[8:16], ohot[1], precision=HIGHEST, preferred_element_type=F32)
    near_res[...] = served[0:NV]
    near_copy = pltpu.make_async_copy(near_res, near_out, near_sem)
    near_copy.start()

    exchange_wait(a1, GX, a2a_send.at[0])
    exchange_wait(bt, GY, a2a_send.at[1])
    exchange_wait(d1, GY, a2a_send.at[2])
    exchange_wait(et, GX, a2a_send.at[3])

    def drain(v, carry):
        for step in range(STEPS):
            for side in range(4):
                @pl.when(sends[side])
                def _():
                    face(step, v, side).wait_send()
        flow_back(v).wait()
        return carry

    lax.fori_loop(0, NV, drain, 0)
    near_copy.wait()


def shards(flow, near, donor_owner, donor_block, recv_offset, weights):
    anywhere = pl.BlockSpec(memory_space=pl.ANY)
    vmem = pltpu.VMEM
    dma = pltpu.SemaphoreType.DMA
    return pl.pallas_call(
        kernel,
        out_shape=(
            jax.ShapeDtypeStruct((NV, CX, CY, CZ), F32),
            jax.ShapeDtypeStruct((NV, FR), F32),
        ),
        in_specs=[anywhere] * 6,
        out_specs=(anywhere, anywhere),
        scratch_shapes=[
            vmem((NV * PX, PY, CZ), F32),
            vmem((NV * PX, PY, CZ), F32),
            vmem((NV * CX, CY, CZ), F32),
            vmem((STEPS, NV, 2, 3, CY, CZ), F32),
            vmem((STEPS, NV, 2, 3 * CX, CZ), F32),
            vmem((STEPS, NV, 2, 3 * CX, CZ), F32),
            vmem((NV, FR), F32),
            vmem((1, FR), jnp.int32),
            vmem((1, FR), jnp.int32),
            vmem((1, FR), jnp.int32),
            vmem((24, FR), F32),
            vmem((NV, FR), F32),
            vmem((GX, GY, 128), F32),
            vmem((GX, GY, 128), F32),
            vmem((GY, GX, 128), F32),
            vmem((GY, GX, 128), F32),
            vmem((GY, GX, 128), F32),
            vmem((GY, GX, 128), F32),
            vmem((GX, GY, 128), F32),
            vmem((GX, GY, 128), F32),
            vmem((2, DEVICES, FR), F32),
            vmem((3 * CZ, SLOTS), BF16),
            vmem((CX * CY, SLOTS), F32),
            vmem((CX * CY, SLOTS), BF16),
            vmem((CZ, 2 * SLOTS), BF16),
            vmem((CX * CY, CZ), F32),
            dma((NV,)),
            dma((5,)),
            dma((STEPS, NV, 4)),
            dma((STEPS, NV, 4)),
            dma((4,)),
            dma((4,)),
            dma((NV,)),
            dma,
        ],
        compiler_params=pltpu.CompilerParams(
            collective_id=0, has_side_effects=True, vmem_limit_bytes=48 * 1024 * 1024
        ),
        cost_estimate=pl.CostEstimate(
            flops=2 * STEPS * 20 * NV * CX * CY * CZ,
            bytes_accessed=2 * 4 * NV * CX * CY * CZ,
            transcendentals=0,
        ),
        name="rotor_wake_steps",
    )(
        flow,
        near,
        donor_owner.reshape(1, FR),
        donor_block.reshape(1, FR),
        recv_offset.reshape(1, FR),
        weights.reshape(24, FR),
    )


def solution(mesh):
    in_specs = (
        P(None, "gx", "gy", None),
        P(None, ("gx", "gy")),
        P(("gx", "gy"), None),
        P(("gx", "gy")),
        P(("gx", "gy")),
        P(None, None, ("gx", "gy")),
    )
    out_specs = (P(None, "gx", "gy", None), P(None, ("gx", "gy")))
    return jax.shard_map(shards, mesh=mesh, in_specs=in_specs, out_specs=out_specs, check_vma=False)
```

time: 325 us -> 48.1 us (0.15)
  local copies, waits for them, and re-layouts: 121 us -> 6.32 us
  waiting for transfers between devices: 75.7 us -> 0 us
  starting transfers between devices: 49 us -> 0 us
  blocking collectives: 45 us -> 0 us
  Pallas kernels: 0 us -> 40.8 us
  other arithmetic: 23.8 us -> 0 us
  matrix products: 7.29 us -> 0 us
    reshape x12 -> x0, local copies, waits for them, and re-layouts: 65.8 us -> none  [the longest x2 27.1 us: to_blocks(): flow.reshape(width_v, cells_x // 8, 8, cells_y // 8, 8, cells_z // 8, 8)]
    all_to_all x4 -> x0, waiting for transfers between devices: 58.3 us -> none  [the longest x1 32.6 us: shards(): lax.all_to_all(picked, ('gx', 'gy'), split_axis=0, concat_axis=0, tiled=T...]
    all_to_all x1 -> x0, blocking collectives: 45 us -> none  [shards(): lax.all_to_all(picked, ('gx', 'gy'), split_axis=0, concat_axis=0, tiled=T...]
    pallas_call x0 -> x1, Pallas kernels: none -> 40.8 us  [shards(): pl.pallas_call(kernel, out_shape=(jax.ShapeDtypeStruct((NV, CX, CY, CZ),...]
    transpose x3 -> x0, local copies, waits for them, and re-layouts: 36.1 us -> none  [the longest x2 36.1 us: to_blocks(): jnp.transpose(shaped, (1, 3, 5, 0, 2, 4, 6)).reshape(-1, width_v, 512)]
    all_to_all x4 -> x0, starting transfers between devices: 29.7 us -> none  [the longest x2 10.7 us: shards(): lax.all_to_all(sending, ('gx', 'gy'), split_axis=0, concat_axis=0, tiled=...]
    ppermute x8 -> x0, starting transfers between devices: 19.2 us -> none  [the longest x4 11.7 us: with_halo(): lax.ppermute(lax.slice_in_dim(block, block.shape[dim] - width, None, axis...]
    ppermute x8 -> x0, waiting for transfers between devices: 17.4 us -> none  [the longest x4 12 us: with_halo(): lax.ppermute(lax.slice_in_dim(block, 0, width, axis=dim), axis, backward)]
  transfers between devices with their start and end apart: 12 -> 0, of which waited for: 10 -> 0; matrix products, arithmetic and copies ran while one was open for 3% -> 0% of each run, Pallas kernels for 0% -> 0%
where the time goes in v1:
time: 48.1 us; the launch traced here: 47.8 us
  Pallas kernels  40.8 us (85%)
  local copies, waits for them, and re-layouts  6.32 us (13%)
  between operations  0.65 us (1%)
    pallas_call x1, Pallas kernels, shards(): pl.pallas_call(kernel, out_shape=(jax.ShapeDtypeStruct((NV, CX, CY, CZ),...  40.8 us
    unnamed x14, local copies, waits for them, and re-layouts  6.32 us

profile of v1, /device:TPU:1, one launch (start us, length us, event | category | flops | bytes accessed | tf_op | source)
XLA Modules:
  0.0 47.8 jit_solution(16467085684267320155)
XLA Ops:
  0.6 0.0 copy-start
  0.6 1.3 %copy-done = f32[5,16,32,128]{3,2,1,0:T(8,128)S(1)} copy-done((f32[5,16,32,128]{3,2,1,0:T(8,128)S(1)}, f32[5,16,32,128]{3,2,1,0:T(8,128)}, u32[]{:S(2)}) %copy-start) | copy-done | bytes 1310744
  1.9 0.0 copy-start.1
  2.0 0.7 %copy-done.1 = f32[3,8,128]{2,1,0:T(8,128)S(1)} copy-done((f32[3,8,128]{2,1,0:T(8,128)S(1)}, f32[3,8,128]{2,1,0:T(8,128)}, u32[]{:S(2)}) %copy-start.1) | copy-done | bytes 12312
  2.7 0.0 copy-start.2
  2.7 0.7 %copy-done.2 = f32[5,128]{1,0:T(8,128)S(1)} copy-done((f32[5,128]{1,0:T(8,128)S(1)}, f32[5,128]{1,0:T(8,128)}, u32[]{:S(2)}) %copy-start.2) | copy-done | bytes 2584
  3.3 0.0 copy-start.3
  3.3 0.7 %copy-done.3 = s32[128,1]{0,1:T(1,128)S(1)} copy-done((s32[128,1]{0,1:T(1,128)S(1)}, s32[128,1]{0,1:T(1,128)}, u32[]{:S(2)}) %copy-start.3) | copy-done | bytes 536
  4.0 0.0 copy-start.4
  4.0 0.7 %copy-done.4 = s32[128]{0:T(128)S(1)} copy-done((s32[128]{0:T(128)S(1)}, s32[128]{0:T(128)}, u32[]{:S(2)}) %copy-start.4) | copy-done | bytes 536
  4.7 0.0 copy-start.5
  4.7 0.7 %copy-done.5 = s32[128]{0:T(128)S(1)} copy-done((s32[128]{0:T(128)S(1)}, s32[128]{0:T(128)}, u32[]{:S(2)}) %copy-start.5) | copy-done | bytes 536
  5.3 40.8 %rotor_wake_steps.1 = (f32[5,16,32,128]{3,2,1,0:T(8,128)S(1)}, f32[5,128]{1,0:T(8,128)S(1)}) custom-call(f32[5,16,32,128]{3,2,1,0:T(8,128)S(1)} %copy-done, f32[5,128]{1,0:T(8,128)S(1)} %copy-done.2, s32[1,128]{1,0:T(1,128)S(1)} %bitcast.5, s32[1,128]{1,0:T(1,128)S(1)} %bitcast.6, s32[1,128]{1,0:T(1,128)S(1)} %bitcast.7, f32[24,128]{1,0:T(8,128)S(1)} %bitcast.4), custom_call_target="tpu_custom_call" | custom-call | flops 26214400 | bytes 2621440 | tf_op jit(solution)/shard_map/rotor_wake_steps/pallas_call | solution.py:423
  46.1 1.1 %copy.10 = f32[5,16,32,128]{3,2,1,0:T(8,128)} copy(f32[5,16,32,128]{3,2,1,0:T(8,128)S(1)} %get-tuple-element.4) | data formatting | bytes 2621440
  47.2 0.6 %copy.11 = f32[5,128]{1,0:T(8,128)} copy(f32[5,128]{1,0:T(8,128)S(1)} %get-tuple-element.5) | data formatting | bytes 5120
Async XLA Ops:
  0.6 1.3 %copy-start = (f32[5,16,32,128]{3,2,1,0:T(8,128)S(1)}, f32[5,16,32,128]{3,2,1,0:T(8,128)}, u32[]{:S(2)}) copy-start(f32[5,16,32,128]{3,2,1,0:T(8,128)} %flow_hbm.1) | copy-start | bytes 3932164
  1.9 0.7 %copy-start.1 = (f32[3,8,128]{2,1,0:T(8,128)S(1)}, f32[3,8,128]{2,1,0:T(8,128)}, u32[]{:S(2)}) copy-start(f32[3,8,128]{2,1,0:T(8,128)} %param.11) | copy-start | bytes 36868
  2.7 0.7 %copy-start.2 = (f32[5,128]{1,0:T(8,128)S(1)}, f32[5,128]{1,0:T(8,128)}, u32[]{:S(2)}) copy-start(f32[5,128]{1,0:T(8,128)} %near_hbm.1) | copy-start | bytes 7684
  3.3 0.7 %copy-start.3 = (s32[128,1]{0,1:T(1,128)S(1)}, s32[128,1]{0,1:T(1,128)}, u32[]{:S(2)}) copy-start(s32[128,1]{0,1:T(1,128)} %param.8) | copy-start | bytes 1540
  4.0 0.7 %copy-start.4 = (s32[128]{0:T(128)S(1)}, s32[128]{0:T(128)}, u32[]{:S(2)}) copy-start(s32[128]{0:T(128)} %param.9) | copy-start | bytes 1540
  4.7 0.7 %copy-start.5 = (s32[128]{0:T(128)S(1)}, s32[128]{0:T(128)}, u32[]{:S(2)}) copy-start(s32[128]{0:T(128)} %param.10) | copy-start | bytes 1540

commit v2 on v1

--- a/solution.py
+++ b/solution.py
@@ -48,13 +48,20 @@
     return high, low
 
 
+def three_term(values, right):
+    high, low = split(values)
+    return jnp.dot(
+        jnp.concatenate([high, low, high], axis=1), right, preferred_element_type=F32
+    )
+
+
 def kernel(
     flow_hbm, near_hbm, owner_hbm, block_hbm, offset_hbm, weights_hbm,
     flow_out, near_out,
     g0, g1, res, hx, hy, sy,
     near_in, owner_in, block_in, offset_in, weights_in, near_res,
     a1, b1, bt, c1, d1, e1, et, fin,
-    ohot, wz_rhs, plane, pick, pzt, recip,
+    ohot, along_z, wz_rhs, plane, pick, pzt, recip,
     in_sem, small_sem, halo_send, halo_recv, a2a_send, a2a_recv, out_sem, near_sem,
 ):
     gx = lax.axis_index("gx")
@@ -108,6 +115,16 @@
         return carry
 
     lax.fori_loop(0, NV, clear, 0)
+
+    z_from = lax.broadcasted_iota(jnp.int32, (CZ, CZ), 0)
+    z_to = lax.broadcasted_iota(jnp.int32, (CZ, CZ), 1)
+    band = jnp.zeros((CZ, CZ), F32)
+    for j in OFFSETS:
+        band = jnp.where(z_from - z_to == j, tap(2, j), band)
+    band_high, band_low = split(band)
+    along_z[0:CZ] = band_high
+    along_z[CZ : 2 * CZ] = band_high
+    along_z[2 * CZ :] = band_low
 
     for copy in small:
         copy.wait()
@@ -220,30 +237,22 @@
 
     lax.fori_loop(0, NV, first_faces, 0)
 
-    lane = lax.broadcasted_iota(jnp.int32, (8, CZ), 1)
-    along_z = [
-        jnp.where((lane + j >= 0) & (lane + j < CZ), tap(2, j), 0.0).astype(F32) for j in OFFSETS
-    ]
-
     def interior(step, low, high):
         g = (g0, g1)[step]
 
-        def body(i, carry):
-            at = (i // CX) * PX + lax.rem(i, CX) + 3
-            mid = g[at, Y0 : Y0 + CY]
+        def body(v, carry):
+            at = v * PX + 3
+            mid = g[pl.ds(at, CX), Y0 : Y0 + CY]
             total = mid * CENTER
             for j in OFFSETS:
-                total = total + g[at + j, Y0 : Y0 + CY] * tap(0, j)
+                total = total + g[pl.ds(at + j, CX), Y0 : Y0 + CY] * tap(0, j)
             for j in OFFSETS:
-                total = total + g[at, Y0 + j : Y0 + CY + j] * tap(1, j)
-            tiles = mid.reshape(CY // 8, 8, CZ)
-            for k, j in enumerate(OFFSETS):
-                moved = pltpu.roll(mid, (-j) % CZ, axis=1).reshape(CY // 8, 8, CZ)
-                total = total + (moved * along_z[k][None]).reshape(CY, CZ)
-            res[i] = total
+                total = total + g[pl.ds(at, CX), Y0 + j : Y0 + CY + j] * tap(1, j)
+            z_part = three_term(mid.reshape(CX * CY, CZ), along_z[...])
+            res[pl.ds(v * CX, CX)] = total + z_part.reshape(CX, CY, CZ)
             return carry
 
-        lax.fori_loop(low * CX, high * CX, body, 0)
+        lax.fori_loop(low, high, body, 0)
 
     interior(0, 0, 2)
 
@@ -327,11 +336,7 @@
                     face(step, v, side).wait_recv()
             add_halo(step, v)
             values = flat_res[pl.ds(pl.multiple_of(v * CX * CY, CX * CY), CX * CY)]
-            high, low = split(values)
-            t = jnp.dot(
-                jnp.concatenate([high, low, high], axis=1), wz_rhs[...],
-                preferred_element_type=F32,
-            )
+            t = three_term(values, wz_rhs[...])
             here = jnp.sum(t * plane[...], axis=0, keepdims=True)
             return jnp.where(row8 == v, here, interp)
 
@@ -417,7 +422,7 @@
 
 
 def shards(flow, near, donor_owner, donor_block, recv_offset, weights):
-    anywhere = pl.BlockSpec(memory_space=pl.ANY)
+    anywhere = pl.BlockSpec(memory_space=pltpu.HBM)
     vmem = pltpu.VMEM
     dma = pltpu.SemaphoreType.DMA
     return pl.pallas_call(
@@ -450,6 +455,7 @@
             vmem((GX, GY, 128), F32),
             vmem((GX, GY, 128), F32),
             vmem((2, DEVICES, FR), F32),
+            vmem((3 * CZ, CZ), BF16),
             vmem((3 * CZ, SLOTS), BF16),
             vmem((CX * CY, SLOTS), F32),
             vmem((CX * CY, SLOTS), BF16),
@@ -465,7 +471,7 @@
             dma,
         ],
         compiler_params=pltpu.CompilerParams(
-            collective_id=0, has_side_effects=True, vmem_limit_bytes=48 * 1024 * 1024
+            collective_id=0, has_side_effects=True, vmem_limit_bytes=60 * 1024 * 1024
         ),
         cost_estimate=pl.CostEstimate(
             flops=2 * STEPS * 20 * NV * CX * CY * CZ,

time: 48.1 us -> 39.1 us (0.81)
  Pallas kernels: 40.8 us -> 35.2 us
  local copies, waits for them, and re-layouts: 6.32 us -> 3.12 us
    pallas_call x1, Pallas kernels: 40.8 us -> 35.2 us  [shards(): pl.pallas_call(kernel, out_shape=(jax.ShapeDtypeStruct((NV, CX, CY, CZ),...]
    unnamed x14 -> x4, local copies, waits for them, and re-layouts: 6.32 us -> 3.12 us
where the time goes in v2:
time: 39.1 us; the launch traced here: 38.9 us
  Pallas kernels  35.2 us (90%)
  local copies, waits for them, and re-layouts  3.12 us (8%)
  between operations  0.65 us (2%)
    pallas_call x1, Pallas kernels, shards(): pl.pallas_call(kernel, out_shape=(jax.ShapeDtypeStruct((NV, CX, CY, CZ),...  35.2 us
    unnamed x4, local copies, waits for them, and re-layouts  3.12 us

profile of v2, /device:TPU:1, one launch (start us, length us, event | category | flops | bytes accessed | tf_op | source)
XLA Modules:
  0.0 38.9 jit_solution(5767082698264094367)
XLA Ops:
  0.6 35.2 %rotor_wake_steps.1 = (f32[5,16,32,128]{3,2,1,0:T(8,128)}, f32[5,128]{1,0:T(8,128)}) custom-call(f32[5,16,32,128]{3,2,1,0:T(8,128)} %flow_hbm.1, f32[5,128]{1,0:T(8,128)} %near_hbm.1, s32[1,128]{1,0:T(1,128)} %bitcast.5, s32[1,128]{1,0:T(1,128)} %bitcast.6, s32[1,128]{1,0:T(1,128)} %bitcast.7, f32[24,128]{1,0:T(8,128)} %bitcast.4), custom_call_target="tpu_custom_call" | custom-call | flops 26214400 | bytes 2621440 | tf_op jit(solution)/shard_map/rotor_wake_steps/pallas_call | solution.py:428
  35.8 0.0 copy-start
  35.8 2.5 %copy.10 = f32[5,16,32,128]{3,2,1,0:T(8,128)} copy(f32[5,16,32,128]{3,2,1,0:T(8,128)} %get-tuple-element.4) | data formatting | bytes 2621440
  38.3 0.0 copy-done
  38.3 0.6 %copy.11 = f32[5,128]{1,0:T(8,128)} copy(f32[5,128]{1,0:T(8,128)S(1)} %copy-done) | data formatting | bytes 5120
Async XLA Ops:
  35.8 2.5 %copy-start = (f32[5,128]{1,0:T(8,128)S(1)}, f32[5,128]{1,0:T(8,128)}, u32[]{:S(2)}) copy-start(f32[5,128]{1,0:T(8,128)} %get-tuple-element.5) | copy-start | bytes 7684

commit v3 on v2

v3 whole, which is shorter than its diff:
```python
import itertools

import jax
import jax.numpy as jnp
from jax import lax
from jax.experimental import pallas as pl
from jax.experimental.pallas import tpu as pltpu
from jax.sharding import PartitionSpec as P

STEPS = 2
NV = 5
CX = 16
CY = 32
CZ = 128
FR = 128
GX = 8
GY = 16
DEVICES = GX * GY
SLOTS = 2 * DEVICES
PX = CX + 6
PY = CY + 16
Y0 = 8

second_taps = (1.0 / 90, -3.0 / 20, 3.0 / 2, -49.0 / 18, 3.0 / 2, -3.0 / 20, 1.0 / 90)
first_taps = (-1.0 / 60, 3.0 / 20, -3.0 / 4, 0.0, 3.0 / 4, -3.0 / 20, 1.0 / 60)
diffusion = 0.05
velocity = (0.6, -0.5, 0.4)
relaxation = 0.6

TAPS = [
    [diffusion * second_taps[o] - velocity[d] * first_taps[o] for o in range(7)] for d in range(3)
]
CENTER = 1.0 + sum(TAPS[d][3] for d in range(3))
OFFSETS = (-3, -2, -1, 1, 2, 3)
HIGHEST = lax.Precision.HIGHEST
MESH = pl.DeviceIdType.MESH
BF16 = jnp.bfloat16
F32 = jnp.float32


OTHERS = sorted(
    itertools.product(range(4), range(2), range(4), range(4)),
    key=lambda o: -10 * sum(min(o[i], 4 - o[i]) for i in (0, 2, 3)) - o[1],
)[:-1]


def tap(dim, j):
    return TAPS[dim][j + 3]


def split(value):
    high = value.astype(BF16)
    low = (value - high.astype(F32)).astype(BF16)
    return high, low


def three_term(values, right):
    high, low = split(values)
    return jnp.dot(
        jnp.concatenate([high, low, high], axis=1), right, preferred_element_type=F32
    )


def kernel(
    flow_hbm, near_hbm, owner_hbm, block_hbm, offset_hbm, weights_hbm,
    flow_out, near_out,
    g0, g1, res, hx, hy, sy,
    near_in, owner_in, block_in, offset_in, weights_in,
    a1, c1, d1, fin,
    ohot, along_z, lhs, wz_rhs, plane, pick, pzt, recip,
    in_sem, small_sem, first_send, first_recv, halo_send, halo_recv, a2a_send, a2a_recv,
):
    gx = lax.axis_index("gx")
    gy = lax.axis_index("gy")
    me = gx * GY + gy
    chip_x, core = gx // 2, lax.rem(gx, 2)
    chip_z, chip_y = gy // 4, lax.rem(gy, 4)

    def others():
        for dx, dc, dz, dy in OTHERS:
            yield (
                lax.rem(chip_x + dx, 4) * 2 + lax.rem(core + dc, 2),
                lax.rem(chip_z + dz, 4) * 4 + lax.rem(chip_y + dy, 4),
            )

    small = [
        pltpu.make_async_copy(src, dst, small_sem.at[i])
        for i, (src, dst) in enumerate(
            (
                (owner_hbm, owner_in),
                (block_hbm, block_in),
                (offset_hbm, offset_in),
                (near_hbm, near_in),
                (weights_hbm, weights_in),
            )
        )
    ]
    for copy in small:
        copy.start()

    def flow_in(v):
        return pltpu.make_async_copy(
            flow_hbm.at[v], g0.at[v, pl.ds(3, CX), pl.ds(Y0, CY)], in_sem.at[v]
        )

    for v in range(NV):
        flow_in(v).start()

    hx[...] = jnp.zeros_like(hx)
    hy[...] = jnp.zeros_like(hy)
    barrier = pltpu.get_barrier_semaphore()
    for peer in others():
        pl.semaphore_signal(barrier, inc=1, device_id=peer, device_id_type=MESH)

    def clear(v, carry):
        for g in (g0, g1):
            g[v, 0:3, Y0 : Y0 + CY] = jnp.zeros((3, CY, CZ), F32)
            g[v, PX - 3 : PX, Y0 : Y0 + CY] = jnp.zeros((3, CY, CZ), F32)
            g[v, 3 : PX - 3, 0:Y0] = jnp.zeros((CX, Y0, CZ), F32)
            g[v, 3 : PX - 3, Y0 + CY : PY] = jnp.zeros((CX, PY - Y0 - CY, CZ), F32)
        return carry

    lax.fori_loop(0, NV, clear, 0)

    z_from = lax.broadcasted_iota(jnp.int32, (CZ, CZ), 0)
    z_to = lax.broadcasted_iota(jnp.int32, (CZ, CZ), 1)
    band = jnp.zeros((CZ, CZ), F32)
    for j in OFFSETS:
        band = jnp.where(z_from - z_to == j, tap(2, j), band)
    band_high, band_low = split(band)
    along_z[0:CZ] = band_high
    along_z[CZ : 2 * CZ] = band_high
    along_z[2 * CZ :] = band_low

    for copy in small:
        copy.wait()
    row = lax.broadcasted_iota(jnp.int32, (FR, FR), 0)
    col = lax.broadcasted_iota(jnp.int32, (FR, FR), 1)
    owner_wide = jnp.broadcast_to(owner_in[...], (FR, FR))
    owner_tall = jnp.transpose(owner_wide)
    earlier = jnp.where((owner_wide == owner_tall) & (row < col), 1.0, 0.0).astype(F32)
    rank = jnp.sum(earlier, axis=0, keepdims=True)
    mine = owner_wide == row
    ohot[0] = jnp.where(mine & (rank < 0.5), 1.0, 0.0).astype(F32)
    ohot[1] = jnp.where(mine & (rank > 0.5), 1.0, 0.0).astype(F32)
    payload = jnp.concatenate(
        [
            weights_in[...],
            near_in[...],
            block_in[...].astype(F32),
            offset_in[...].astype(F32),
            jnp.ones((1, FR), F32),
        ],
        axis=0,
    )
    nothing = jnp.zeros((32, FR), F32)
    blank = jnp.zeros((64, FR), F32)
    contract_last = (((1,), (1,)), ((), ()))
    a1[...] = lax.dot_general(
        ohot[0], jnp.concatenate([payload, nothing, blank], axis=0), contract_last,
        precision=HIGHEST, preferred_element_type=F32,
    ) + lax.dot_general(
        ohot[1], jnp.concatenate([nothing, payload, blank], axis=0), contract_last,
        precision=HIGHEST, preferred_element_type=F32,
    )

    targets = ((gx + 1, gy), (gx - 1, gy), (gx, gy + 1), (gx, gy - 1))
    sends = (gx < GX - 1, gx > 0, gy < GY - 1, gy > 0)
    takes = (gx > 0, gx < GX - 1, gy > 0, gy < GY - 1)

    def face(step, side, v=None):
        g = (g0, g1)[step]
        if side < 2:
            layers = pl.ds(CX if side == 0 else 3, 3)
            if v is None:
                src, dst = g.at[:, layers, pl.ds(Y0, CY)], hx.at[step, side]
            else:
                src, dst = g.at[v, layers, pl.ds(Y0, CY)], hx.at[step, side, v]
        elif v is None:
            src, dst = sy.at[step, side - 2], hy.at[step, side - 2]
        else:
            src, dst = sy.at[step, side - 2, v], hy.at[step, side - 2, v]
        return pltpu.make_async_remote_copy(
            src_ref=src, dst_ref=dst,
            send_sem=first_send.at[side] if v is None else halo_send.at[v, side],
            recv_sem=first_recv.at[side] if v is None else halo_recv.at[v, side],
            device_id=targets[side], device_id_type=MESH,
        )

    def pack_faces(step, v):
        flat = (g0, g1)[step].reshape(NV * PX * PY, CZ)
        for side, first in ((0, CY - 3), (1, 0)):
            for j in range(3):
                for half in range(2):
                    start = (v * PX + 3 + 8 * half) * PY + Y0 + first + j
                    sy[step, side, v, pl.ds(j * CX + 8 * half, 8)] = flat[pl.ds(start, 8, PY)]

    def interior(step):
        g = (g0, g1)[step]

        def body(v, carry):
            if step == 0:
                flow_in(v).wait()
                pack_faces(0, v)
            mid = g[v, 3 : 3 + CX, Y0 : Y0 + CY]
            total = mid * CENTER
            for j in OFFSETS:
                total = total + g[v, 3 + j : 3 + j + CX, Y0 : Y0 + CY] * tap(0, j)
            for j in OFFSETS:
                total = total + g[v, 3 : 3 + CX, Y0 + j : Y0 + CY + j] * tap(1, j)
            z_part = three_term(mid.reshape(CX * CY, CZ), along_z[...])
            res[pl.ds(v * CX, CX)] = total + z_part.reshape(CX, CY, CZ)
            return carry

        lax.fori_loop(0, NV, body, 0)

    interior(0)

    def exchange(src, dst, phase):
        for px, py in others():
            pltpu.make_async_remote_copy(
                src_ref=src.at[pl.ds(px * GY + py, 1)], dst_ref=dst.at[pl.ds(me, 1)],
                send_sem=a2a_send.at[phase], recv_sem=a2a_recv.at[phase],
                device_id=(px, py), device_id_type=MESH,
            ).start()
        dst[pl.ds(me, 1)] = src[pl.ds(me, 1)]

    def exchange_wait(buf, sem):
        part = buf.at[pl.ds(0, DEVICES - 1)]
        pltpu.make_async_copy(part, part, sem).wait()

    pl.semaphore_wait(barrier, DEVICES - 1)
    for side in range(4):
        @pl.when(sends[side])
        def _():
            face(0, side).start()
    exchange(a1, c1, 0)

    flat_res = res.reshape(NV * CX * CY, CZ)

    def add_halo(step, v):
        for r in range(3):
            low = res[v * CX + r]
            high = res[v * CX + CX - 1 - r]
            for j in range(-3, -r):
                low = low + hx[step, 0, v, r + j + 3] * tap(0, j)
                high = high + hx[step, 1, v, -r - 1 - j] * tap(0, -j)
            res[v * CX + r] = low
            res[v * CX + CX - 1 - r] = high
        for r in range(3):
            for half in range(2):
                start = (v * CX + 8 * half) * CY
                at_low = pl.ds(start + r, 8, CY)
                at_high = pl.ds(start + CY - 1 - r, 8, CY)
                low = flat_res[at_low]
                high = flat_res[at_high]
                for j in range(-3, -r):
                    low = low + hy[step, 0, v, pl.ds((r + j + 3) * CX + 8 * half, 8)] * tap(1, j)
                    high = high + hy[step, 1, v, pl.ds((-r - 1 - j) * CX + 8 * half, 8)] * tap(1, -j)
                flat_res[at_low] = low
                flat_res[at_high] = high

    def variable(v):
        return pl.ds(pl.multiple_of(v * CX * CY, CX * CY), CX * CY)

    for side in range(4):
        @pl.when(takes[side])
        def _():
            face(0, side).wait_recv()

    def first_lhs(v, carry):
        add_halo(0, v)
        high, low = split(flat_res[variable(v)])
        lhs[variable(v), 0:CZ] = high
        lhs[variable(v), CZ : 2 * CZ] = low
        lhs[variable(v), 2 * CZ :] = high
        return carry

    lax.fori_loop(0, NV, first_lhs, 0)

    exchange_wait(c1, a2a_recv.at[0])
    table = jnp.transpose(c1[...])
    asked = jnp.concatenate([table[0:32], table[32:64]], axis=1)
    wx = asked[0:8]
    wy = asked[8:16]
    wz = asked[16:24]
    last = asked[24:32]
    block = last[5:6].astype(jnp.int32)
    offset = last[6:7].astype(jnp.int32)
    live = last[7:8]
    row8 = lax.broadcasted_iota(jnp.int32, (8, SLOTS), 0)
    near = jnp.where(row8 < NV, last, 0.0)
    kx = block // 64
    ky = (block // 16) % 4
    kz = block % 16
    weights_z = jnp.concatenate(
        [jnp.where(kz == b, wz, 0.0) for b in range(CZ // 8)], axis=0
    )
    z_high, z_low = split(weights_z)
    wz_rhs[0:CZ] = z_high
    wz_rhs[CZ : 2 * CZ] = z_high
    wz_rhs[2 * CZ :] = z_low
    weights_x = jnp.concatenate([jnp.where(kx == b, wx, 0.0) for b in range(CX // 8)], axis=0)
    weights_y = jnp.concatenate([jnp.where(ky == b, wy, 0.0) for b in range(CY // 8)], axis=0)
    for x in range(CX):
        plane[x * CY : (x + 1) * CY] = weights_x[x : x + 1] * weights_y
    cell = (8 * kx + offset // 64) * CY + 8 * ky + (offset // 8) % 8
    cell = jnp.where(live > 0.5, cell, -1)
    cell_z = 8 * kz + offset % 8
    places = lax.broadcasted_iota(jnp.int32, (CX * CY, SLOTS), 0)
    pick[...] = jnp.where(places == cell, 1.0, 0.0).astype(F32).astype(BF16)
    places_z = lax.broadcasted_iota(jnp.int32, (CZ, SLOTS), 0)
    hot_z = jnp.where(places_z == cell_z, 1.0, 0.0).astype(F32).astype(BF16)
    pzt[:, 0:SLOTS] = hot_z
    pzt[:, SLOTS:] = hot_z
    counts = lax.dot_general(
        pick[...], hot_z, contract_last, preferred_element_type=F32
    )
    recip[...] = 1.0 / (1.0 + counts)

    def relaxed(step, near):
        def body(v, interp):
            if step == 0:
                t = jnp.dot(lhs[variable(v)], wz_rhs[...], preferred_element_type=F32)
            else:
                for side in range(4):
                    @pl.when(takes[side])
                    def _():
                        face(1, side, v).wait_recv()
                add_halo(1, v)
                t = three_term(flat_res[variable(v)], wz_rhs[...])
            here = jnp.sum(t * plane[...], axis=0, keepdims=True)
            return jnp.where(row8 == v, here, interp)

        interp = lax.fori_loop(0, NV, body, jnp.zeros((8, SLOTS), F32))
        return near + relaxation * (interp - near)

    def injected(v, near):
        here = jnp.sum(jnp.where(row8 == v, near, 0.0), axis=0, keepdims=True)
        here = jnp.broadcast_to(here, (16, SLOTS))
        high, low = split(here)
        hot = pick[...].reshape(CX * CY // 16, 16, SLOTS)
        left = jnp.concatenate(
            [
                (hot * high[None]).reshape(CX * CY, SLOTS),
                (hot * low[None]).reshape(CX * CY, SLOTS),
            ],
            axis=1,
        )
        gained = lax.dot_general(left, pzt[...], contract_last, preferred_element_type=F32)
        return ((flat_res[variable(v)] + gained) * recip[...]).reshape(CX, CY, CZ)

    near = relaxed(0, near)

    def second_faces(v, carry):
        g1[v, 3 : 3 + CX, Y0 : Y0 + CY] = injected(v, near)
        pack_faces(1, v)
        for side in range(4):
            @pl.when(sends[side])
            def _():
                face(1, side, v).start()
        return carry

    lax.fori_loop(0, NV, second_faces, 0)
    interior(1)
    near = relaxed(1, near)

    back = jnp.concatenate(
        [near[:, :DEVICES], near[:, DEVICES:], jnp.zeros((DEVICES - 16, DEVICES), F32)], axis=0
    )
    d1[...] = jnp.transpose(back)
    exchange(d1, fin, 1)

    def last_injection(v, carry):
        flow_out[v] = injected(v, near)
        return carry

    lax.fori_loop(0, NV, last_injection, 0)

    exchange_wait(a1, a2a_send.at[0])
    for side in range(4):
        @pl.when(sends[side])
        def _():
            face(0, side).wait_send()

    def drain(v, carry):
        for side in range(4):
            @pl.when(sends[side])
            def _():
                face(1, side, v).wait_send()
        return carry

    lax.fori_loop(0, NV, drain, 0)
    exchange_wait(d1, a2a_send.at[1])
    exchange_wait(fin, a2a_recv.at[1])
    returned = jnp.transpose(fin[...])
    served = jnp.dot(
        returned[0:8], ohot[0], precision=HIGHEST, preferred_element_type=F32
    ) + jnp.dot(returned[8:16], ohot[1], precision=HIGHEST, preferred_element_type=F32)
    near_out[...] = served[0:NV]


def hand_over(flow_vmem, near_vmem, flow_out, near_out, sems):
    copies = [
        pltpu.make_async_copy(flow_vmem, flow_out, sems.at[0]),
        pltpu.make_async_copy(near_vmem, near_out, sems.at[1]),
    ]
    for copy in copies:
        copy.start()
    for copy in copies:
        copy.wait()


def shards(flow, near, donor_owner, donor_block, recv_offset, weights):
    hbm = pl.BlockSpec(memory_space=pltpu.HBM)
    whole = pl.BlockSpec(memory_space=pltpu.VMEM)
    vmem = pltpu.VMEM
    dma = pltpu.SemaphoreType.DMA
    operands = (
        flow,
        near,
        donor_owner.reshape(1, FR),
        donor_block.reshape(1, FR),
        recv_offset.reshape(1, FR),
        weights.reshape(24, FR),
    )
    flow, near = pl.pallas_call(
        kernel,
        out_shape=(vmem((NV, CX, CY, CZ), F32), vmem((NV, FR), F32)),
        in_specs=[hbm] * 6,
        out_specs=(whole, whole),
        scratch_shapes=[
            vmem((NV, PX, PY, CZ), F32),
            vmem((NV, PX, PY, CZ), F32),
            vmem((NV * CX, CY, CZ), F32),
            vmem((STEPS, 2, NV, 3, CY, CZ), F32),
            vmem((STEPS, 2, NV, 3 * CX, CZ), F32),
            vmem((STEPS, 2, NV, 3 * CX, CZ), F32),
            vmem((NV, FR), F32),
            vmem((1, FR), jnp.int32),
            vmem((1, FR), jnp.int32),
            vmem((1, FR), jnp.int32),
            vmem((24, FR), F32),
            vmem((DEVICES, 128), F32),
            vmem((DEVICES, 128), F32),
            vmem((DEVICES, 128), F32),
            vmem((DEVICES, 128), F32),
            vmem((2, DEVICES, FR), F32),
            vmem((3 * CZ, CZ), BF16),
            vmem((NV * CX * CY, 3 * CZ), BF16),
            vmem((3 * CZ, SLOTS), BF16),
            vmem((CX * CY, SLOTS), F32),
            vmem((CX * CY, SLOTS), BF16),
            vmem((CZ, 2 * SLOTS), BF16),
            vmem((CX * CY, CZ), F32),
            dma((NV,)),
            dma((5,)),
            dma((4,)),
            dma((4,)),
            dma((NV, 4)),
            dma((NV, 4)),
            dma((2,)),
            dma((2,)),
        ],
        compiler_params=pltpu.CompilerParams(
            collective_id=0, has_side_effects=True, vmem_limit_bytes=40 * 1024 * 1024
        ),
        cost_estimate=pl.CostEstimate(
            flops=2 * STEPS * 20 * NV * CX * CY * CZ,
            bytes_accessed=2 * 4 * NV * CX * CY * CZ,
            transcendentals=0,
        ),
        name="rotor_wake_steps",
    )(*[pltpu.with_memory_space_constraint(operand, pltpu.HBM) for operand in operands])
    return pl.pallas_call(
        hand_over,
        out_shape=(
            jax.ShapeDtypeStruct((NV, CX, CY, CZ), F32),
            jax.ShapeDtypeStruct((NV, FR), F32),
        ),
        in_specs=[whole, whole],
        out_specs=(hbm, hbm),
        scratch_shapes=[dma((2,))],
        name="hand_over",
    )(
        pltpu.with_memory_space_constraint(flow, pltpu.VMEM),
        pltpu.with_memory_space_constraint(near, pltpu.VMEM),
    )


def solution(mesh):
    in_specs = (
        P(None, "gx", "gy", None),
        P(None, ("gx", "gy")),
        P(("gx", "gy"), None),
        P(("gx", "gy")),
        P(("gx", "gy")),
        P(None, None, ("gx", "gy")),
    )
    out_specs = (P(None, "gx", "gy", None), P(None, ("gx", "gy")))
    return jax.shard_map(shards, mesh=mesh, in_specs=in_specs, out_specs=out_specs, check_vma=False)
```

time: 39.1 us -> 34.9 us (0.89)
  local copies, waits for them, and re-layouts: 3.12 us -> 0 us
  Pallas kernels: 35.2 us -> 34.2 us
    unnamed x4 -> x0, local copies, waits for them, and re-layouts: 3.12 us -> none
    pallas_call x1 -> x2, Pallas kernels: 35.2 us -> 34.2 us  [the longest x1 33.1 us: shards(): pl.pallas_call(kernel, out_shape=(vmem((NV, CX, CY, CZ), F32), vmem((NV,...]
where the time goes in v3:
time: 34.9 us; the launch traced here: 34.8 us
  Pallas kernels  34.2 us (98%)
  between operations  0.64 us (2%)
    pallas_call x1, Pallas kernels, shards(): pl.pallas_call(kernel, out_shape=(vmem((NV, CX, CY, CZ), F32), vmem((NV,...  33.1 us
    pallas_call x1, Pallas kernels, shards(): pl.pallas_call(hand_over, out_shape=(jax.ShapeDtypeStruct((NV, CX, CY, CZ...  1.08 us

profile of v3, /device:TPU:1, one launch (start us, length us, event | category | flops | bytes accessed | tf_op | source)
XLA Modules:
  0.0 34.8 jit_solution(11572974958807807555)
XLA Ops:
  0.6 33.1 %rotor_wake_steps.1 = (f32[5,16,32,128]{3,2,1,0:T(8,128)S(1)}, f32[5,128]{1,0:T(8,128)S(1)}) custom-call(f32[5,16,32,128]{3,2,1,0:T(8,128)} %flow_hbm.1, f32[5,128]{1,0:T(8,128)} %near_hbm.1, s32[1,128]{1,0:T(1,128)} %bitcast.5, s32[1,128]{1,0:T(1,128)} %bitcast.6, s32[1,128]{1,0:T(1,128)} %bitcast.7, f32[24,128]{1,0:T(8,128)} %bitcast.4), custom_call_target="tpu_custom_call" | custom-call | flops 26214400 | bytes 2621440 | tf_op jit(solution)/shard_map/rotor_wake_steps/pallas_call | solution.py:427
  33.7 1.1 %hand_over.1 = (f32[5,16,32,128]{3,2,1,0:T(8,128)}, f32[5,128]{1,0:T(8,128)}) custom-call(f32[5,16,32,128]{3,2,1,0:T(8,128)S(1)} %get-tuple-element.4.flow_vmem, f32[5,128]{1,0:T(8,128)S(1)} %get-tuple-element.5.near_vmem), custom_call_target="tpu_custom_call" | custom-call | tf_op jit(solution)/shard_map/hand_over/pallas_call | solution.py:475

commit v4 on v3

--- a/solution.py
+++ b/solution.py
@@ -83,6 +83,12 @@
                 lax.rem(chip_z + dz, 4) * 4 + lax.rem(chip_y + dy, 4),
             )
 
+    barrier = pltpu.get_barrier_semaphore()
+    peers = list(others())
+
+    for peer in peers:
+        pl.semaphore_signal(barrier, inc=1, device_id=peer, device_id_type=MESH)
+
     small = [
         pltpu.make_async_copy(src, dst, small_sem.at[i])
         for i, (src, dst) in enumerate(
@@ -105,12 +111,6 @@
 
     for v in range(NV):
         flow_in(v).start()
-
-    hx[...] = jnp.zeros_like(hx)
-    hy[...] = jnp.zeros_like(hy)
-    barrier = pltpu.get_barrier_semaphore()
-    for peer in others():
-        pl.semaphore_signal(barrier, inc=1, device_id=peer, device_id_type=MESH)
 
     def clear(v, carry):
         for g in (g0, g1):
@@ -187,6 +187,13 @@
             device_id=targets[side], device_id_type=MESH,
         )
 
+    for side in range(4):
+        @pl.when(jnp.logical_not(takes[side]))
+        def _():
+            halo = (hx, hx, hy, hy)[side]
+            for step in range(STEPS):
+                halo[step, side % 2] = jnp.zeros(halo.shape[2:], F32)
+
     def pack_faces(step, v):
         flat = (g0, g1)[step].reshape(NV * PX * PY, CZ)
         for side, first in ((0, CY - 3), (1, 0)):
@@ -199,9 +206,6 @@
         g = (g0, g1)[step]
 
         def body(v, carry):
-            if step == 0:
-                flow_in(v).wait()
-                pack_faces(0, v)
             mid = g[v, 3 : 3 + CX, Y0 : Y0 + CY]
             total = mid * CENTER
             for j in OFFSETS:
@@ -214,27 +218,32 @@
 
         lax.fori_loop(0, NV, body, 0)
 
-    interior(0)
-
     def exchange(src, dst, phase):
-        for px, py in others():
+        for px, py in peers:
             pltpu.make_async_remote_copy(
                 src_ref=src.at[pl.ds(px * GY + py, 1)], dst_ref=dst.at[pl.ds(me, 1)],
                 send_sem=a2a_send.at[phase], recv_sem=a2a_recv.at[phase],
                 device_id=(px, py), device_id_type=MESH,
             ).start()
-        dst[pl.ds(me, 1)] = src[pl.ds(me, 1)]
 
     def exchange_wait(buf, sem):
         part = buf.at[pl.ds(0, DEVICES - 1)]
         pltpu.make_async_copy(part, part, sem).wait()
 
+    def first_faces(v, carry):
+        flow_in(v).wait()
+        pack_faces(0, v)
+        return carry
+
+    lax.fori_loop(0, NV, first_faces, 0)
+    c1[pl.ds(me, 1)] = a1[pl.ds(me, 1)]
     pl.semaphore_wait(barrier, DEVICES - 1)
+    exchange(a1, c1, 0)
     for side in range(4):
         @pl.when(sends[side])
         def _():
             face(0, side).start()
-    exchange(a1, c1, 0)
+    interior(0)
 
     flat_res = res.reshape(NV * CX * CY, CZ)
 
@@ -332,7 +341,7 @@
             here = jnp.sum(t * plane[...], axis=0, keepdims=True)
             return jnp.where(row8 == v, here, interp)
 
-        interp = lax.fori_loop(0, NV, body, jnp.zeros((8, SLOTS), F32))
+        interp = lax.fori_loop(0, NV, body, jnp.zeros((8, SLOTS), F32), unroll=True)
         return near + relaxation * (interp - near)
 
     def injected(v, near):
@@ -361,7 +370,7 @@
                 face(1, side, v).start()
         return carry
 
-    lax.fori_loop(0, NV, second_faces, 0)
+    lax.fori_loop(0, NV, second_faces, 0, unroll=True)
     interior(1)
     near = relaxed(1, near)
 
@@ -370,12 +379,13 @@
     )
     d1[...] = jnp.transpose(back)
     exchange(d1, fin, 1)
+    fin[pl.ds(me, 1)] = d1[pl.ds(me, 1)]
 
     def last_injection(v, carry):
         flow_out[v] = injected(v, near)
         return carry
 
-    lax.fori_loop(0, NV, last_injection, 0)
+    lax.fori_loop(0, NV, last_injection, 0, unroll=True)
 
     exchange_wait(a1, a2a_send.at[0])
     for side in range(4):

time: 34.9 us -> 33.3 us (0.954)
  Pallas kernels: 34.2 us -> 32.5 us
    pallas_call x1, Pallas kernels: 33.1 us -> 31.5 us  [shards(): pl.pallas_call(kernel, out_shape=(vmem((NV, CX, CY, CZ), F32), vmem((NV,...]
where the time goes in v4:
time: 33.3 us; the launch traced here: 33.2 us
  Pallas kernels  32.5 us (98%)
  between operations  0.64 us (2%)
    pallas_call x1, Pallas kernels, shards(): pl.pallas_call(kernel, out_shape=(vmem((NV, CX, CY, CZ), F32), vmem((NV,...  31.5 us
    pallas_call x1, Pallas kernels, shards(): pl.pallas_call(hand_over, out_shape=(jax.ShapeDtypeStruct((NV, CX, CY, CZ...  1.08 us

profile of v4, /device:TPU:1, one launch (start us, length us, event | category | flops | bytes accessed | tf_op | source)
XLA Modules:
  0.0 33.2 jit_solution(3001183879601797613)
XLA Ops:
  0.6 31.5 %rotor_wake_steps.1 = (f32[5,16,32,128]{3,2,1,0:T(8,128)S(1)}, f32[5,128]{1,0:T(8,128)S(1)}) custom-call(f32[5,16,32,128]{3,2,1,0:T(8,128)} %flow_hbm.1, f32[5,128]{1,0:T(8,128)} %near_hbm.1, s32[1,128]{1,0:T(1,128)} %bitcast.5, s32[1,128]{1,0:T(1,128)} %bitcast.6, s32[1,128]{1,0:T(1,128)} %bitcast.7, f32[24,128]{1,0:T(8,128)} %bitcast.4), custom_call_target="tpu_custom_call" | custom-call | flops 26214400 | bytes 2621440 | tf_op jit(solution)/shard_map/rotor_wake_steps/pallas_call | solution.py:437
  32.1 1.1 %hand_over.1 = (f32[5,16,32,128]{3,2,1,0:T(8,128)}, f32[5,128]{1,0:T(8,128)}) custom-call(f32[5,16,32,128]{3,2,1,0:T(8,128)S(1)} %get-tuple-element.4.flow_vmem, f32[5,128]{1,0:T(8,128)S(1)} %get-tuple-element.5.near_vmem), custom_call_target="tpu_custom_call" | custom-call | tf_op jit(solution)/shard_map/hand_over/pallas_call | solution.py:485

commit v5 on v4

--- a/solution.py
+++ b/solution.py
@@ -66,9 +66,9 @@
     flow_out, near_out,
     g0, g1, res, hx, hy, sy,
     near_in, owner_in, block_in, offset_in, weights_in,
-    a1, c1, d1, fin,
-    ohot, along_z, lhs, wz_rhs, plane, pick, pzt, recip,
-    in_sem, small_sem, first_send, first_recv, halo_send, halo_recv, a2a_send, a2a_recv,
+    a1, b1, bt, c1, d1, fin,
+    ohot, band_z, lhs, wz_rhs, plane, pick, pzt, recip,
+    in_sem, small_sem, first_send, first_recv, halo_send, halo_recv, row_send, row_recv, vouched,
 ):
     gx = lax.axis_index("gx")
     gy = lax.axis_index("gy")
@@ -83,11 +83,25 @@
                 lax.rem(chip_z + dz, 4) * 4 + lax.rem(chip_y + dy, 4),
             )
 
+    along_x = [(lax.rem(gx + k, GX), gy) for k in range(1, GX)]
+    along_y = [(gx, chip_z * 4 + lax.rem(chip_y + k, 4)) for k in range(1, 4)]
+    along_z = [(gx, lax.rem(gy + 4 * k, GY)) for k in range(1, 4)]
+    plane_yz = [(gx, lax.rem(gy + k, GY)) for k in range(1, GY)]
     barrier = pltpu.get_barrier_semaphore()
-    peers = list(others())
-
-    for peer in peers:
+    for peer in along_y + along_z + along_x:
         pl.semaphore_signal(barrier, inc=1, device_id=peer, device_id_type=MESH)
+    after = (chip_y == 3) & (gy < GY - 1)
+    before = (chip_y == 0) & (gy > 0)
+
+    @pl.when(after)
+    def _():
+        pl.semaphore_signal(barrier, inc=1, device_id=(gx, gy + 1), device_id_type=MESH)
+
+    @pl.when(before)
+    def _():
+        pl.semaphore_signal(barrier, inc=1, device_id=(gx, gy - 1), device_id_type=MESH)
+
+    greeted = GX + 5 + after.astype(jnp.int32) + before.astype(jnp.int32)
 
     small = [
         pltpu.make_async_copy(src, dst, small_sem.at[i])
@@ -128,9 +142,9 @@
     for j in OFFSETS:
         band = jnp.where(z_from - z_to == j, tap(2, j), band)
     band_high, band_low = split(band)
-    along_z[0:CZ] = band_high
-    along_z[CZ : 2 * CZ] = band_high
-    along_z[2 * CZ :] = band_low
+    band_z[0:CZ] = band_high
+    band_z[CZ : 2 * CZ] = band_high
+    band_z[2 * CZ :] = band_low
 
     for copy in small:
         copy.wait()
@@ -212,22 +226,21 @@
                 total = total + g[v, 3 + j : 3 + j + CX, Y0 : Y0 + CY] * tap(0, j)
             for j in OFFSETS:
                 total = total + g[v, 3 : 3 + CX, Y0 + j : Y0 + CY + j] * tap(1, j)
-            z_part = three_term(mid.reshape(CX * CY, CZ), along_z[...])
+            z_part = three_term(mid.reshape(CX * CY, CZ), band_z[...])
             res[pl.ds(v * CX, CX)] = total + z_part.reshape(CX, CY, CZ)
             return carry
 
         lax.fori_loop(0, NV, body, 0)
 
-    def exchange(src, dst, phase):
-        for px, py in peers:
-            pltpu.make_async_remote_copy(
-                src_ref=src.at[pl.ds(px * GY + py, 1)], dst_ref=dst.at[pl.ds(me, 1)],
-                send_sem=a2a_send.at[phase], recv_sem=a2a_recv.at[phase],
-                device_id=(px, py), device_id_type=MESH,
-            ).start()
-
-    def exchange_wait(buf, sem):
-        part = buf.at[pl.ds(0, DEVICES - 1)]
+    def rows_to(src, source, count, dst, target, phase, peer):
+        pltpu.make_async_remote_copy(
+            src_ref=src.at[pl.ds(source, count)], dst_ref=dst.at[pl.ds(target, count)],
+            send_sem=row_send.at[phase], recv_sem=row_recv.at[phase],
+            device_id=peer, device_id_type=MESH,
+        ).start()
+
+    def rows_wait(buf, count, sem):
+        part = buf.at[pl.ds(0, count)]
         pltpu.make_async_copy(part, part, sem).wait()
 
     def first_faces(v, carry):
@@ -236,14 +249,26 @@
         return carry
 
     lax.fori_loop(0, NV, first_faces, 0)
-    c1[pl.ds(me, 1)] = a1[pl.ds(me, 1)]
-    pl.semaphore_wait(barrier, DEVICES - 1)
-    exchange(a1, c1, 0)
+    x_rows = pl.ds(pl.multiple_of(gx * GY, GY), GY)
+    b1[x_rows] = a1[x_rows]
+    pl.semaphore_wait(barrier, greeted)
+    for peer in along_x:
+        rows_to(a1, pl.multiple_of(peer[0] * GY, GY), GY, b1, pl.multiple_of(gx * GY, GY), 0, peer)
+    for peer in along_y:
+        pl.semaphore_signal(vouched, inc=1, device_id=peer, device_id_type=MESH)
     for side in range(4):
         @pl.when(sends[side])
         def _():
             face(0, side).start()
     interior(0)
+    rows_wait(b1, DEVICES - GY, row_recv.at[0])
+    for h in range(GY):
+        bt[h * GX : (h + 1) * GX] = b1[pl.ds(h, GX, GY)]
+    y_rows = pl.ds(pl.multiple_of(gy * GX, GX), GX)
+    c1[y_rows] = bt[y_rows]
+    pl.semaphore_wait(vouched, 3)
+    for peer in plane_yz:
+        rows_to(bt, pl.multiple_of(peer[1] * GX, GX), GX, c1, pl.multiple_of(gy * GX, GX), 1, peer)
 
     flat_res = res.reshape(NV * CX * CY, CZ)
 
@@ -287,7 +312,7 @@
 
     lax.fori_loop(0, NV, first_lhs, 0)
 
-    exchange_wait(c1, a2a_recv.at[0])
+    rows_wait(c1, DEVICES - GX, row_recv.at[1])
     table = jnp.transpose(c1[...])
     asked = jnp.concatenate([table[0:32], table[32:64]], axis=1)
     wx = asked[0:8]
@@ -378,8 +403,9 @@
         [near[:, :DEVICES], near[:, DEVICES:], jnp.zeros((DEVICES - 16, DEVICES), F32)], axis=0
     )
     d1[...] = jnp.transpose(back)
-    exchange(d1, fin, 1)
-    fin[pl.ds(me, 1)] = d1[pl.ds(me, 1)]
+    for px, py in others():
+        rows_to(d1, py * GX + px, 1, fin, me, 2, (px, py))
+    fin[pl.ds(me, 1)] = d1[pl.ds(gy * GX + gx, 1)]
 
     def last_injection(v, carry):
         flow_out[v] = injected(v, near)
@@ -387,7 +413,8 @@
 
     lax.fori_loop(0, NV, last_injection, 0, unroll=True)
 
-    exchange_wait(a1, a2a_send.at[0])
+    rows_wait(a1, DEVICES - GY, row_send.at[0])
+    rows_wait(bt, DEVICES - GX, row_send.at[1])
     for side in range(4):
         @pl.when(sends[side])
         def _():
@@ -401,8 +428,8 @@
         return carry
 
     lax.fori_loop(0, NV, drain, 0)
-    exchange_wait(d1, a2a_send.at[1])
-    exchange_wait(fin, a2a_recv.at[1])
+    rows_wait(d1, DEVICES - 1, row_send.at[2])
+    rows_wait(fin, DEVICES - 1, row_recv.at[2])
     returned = jnp.transpose(fin[...])
     served = jnp.dot(
         returned[0:8], ohot[0], precision=HIGHEST, preferred_element_type=F32
@@ -455,6 +482,8 @@
             vmem((DEVICES, 128), F32),
             vmem((DEVICES, 128), F32),
             vmem((DEVICES, 128), F32),
+            vmem((DEVICES, 128), F32),
+            vmem((DEVICES, 128), F32),
             vmem((2, DEVICES, FR), F32),
             vmem((3 * CZ, CZ), BF16),
             vmem((NV * CX * CY, 3 * CZ), BF16),
@@ -469,8 +498,9 @@
             dma((4,)),
             dma((NV, 4)),
             dma((NV, 4)),
-            dma((2,)),
-            dma((2,)),
+            dma((3,)),
+            dma((3,)),
+            pltpu.SemaphoreType.REGULAR,
         ],
         compiler_params=pltpu.CompilerParams(
             collective_id=0, has_side_effects=True, vmem_limit_bytes=40 * 1024 * 1024

time: 33.3 us -> 32.3 us (0.970)
  Pallas kernels: 32.5 us -> 31.6 us
    pallas_call x1, Pallas kernels: 31.5 us -> 30.5 us  [shards(): pl.pallas_call(kernel, out_shape=(vmem((NV, CX, CY, CZ), F32), vmem((NV,...]
where the time goes in v5:
time: 32.3 us; the launch traced here: 32.2 us
  Pallas kernels  31.6 us (98%)
  between operations  0.64 us (2%)
    pallas_call x1, Pallas kernels, shards(): pl.pallas_call(kernel, out_shape=(vmem((NV, CX, CY, CZ), F32), vmem((NV,...  30.5 us
    pallas_call x1, Pallas kernels, shards(): pl.pallas_call(hand_over, out_shape=(jax.ShapeDtypeStruct((NV, CX, CY, CZ...  1.08 us

profile of v5, /device:TPU:1, one launch (start us, length us, event | category | flops | bytes accessed | tf_op | source)
XLA Modules:
  0.0 32.2 jit_solution(1226956267239852773)
XLA Ops:
  0.6 30.5 %rotor_wake_steps.1 = (f32[5,16,32,128]{3,2,1,0:T(8,128)S(1)}, f32[5,128]{1,0:T(8,128)S(1)}) custom-call(f32[5,16,32,128]{3,2,1,0:T(8,128)} %flow_hbm.1, f32[5,128]{1,0:T(8,128)} %near_hbm.1, s32[1,128]{1,0:T(1,128)} %bitcast.5, s32[1,128]{1,0:T(1,128)} %bitcast.6, s32[1,128]{1,0:T(1,128)} %bitcast.7, f32[24,128]{1,0:T(8,128)} %bitcast.4), custom_call_target="tpu_custom_call" | custom-call | flops 26214400 | bytes 2621440 | tf_op jit(solution)/shard_map/rotor_wake_steps/pallas_call | solution.py:464
  31.1 1.1 %hand_over.1 = (f32[5,16,32,128]{3,2,1,0:T(8,128)}, f32[5,128]{1,0:T(8,128)}) custom-call(f32[5,16,32,128]{3,2,1,0:T(8,128)S(1)} %get-tuple-element.4.flow_vmem, f32[5,128]{1,0:T(8,128)S(1)} %get-tuple-element.5.near_vmem), custom_call_target="tpu_custom_call" | custom-call | tf_op jit(solution)/shard_map/hand_over/pallas_call | solution.py:515

commit v6 on v5

--- a/solution.py
+++ b/solution.py
@@ -66,9 +66,10 @@
     flow_out, near_out,
     g0, g1, res, hx, hy, sy,
     near_in, owner_in, block_in, offset_in, weights_in,
-    a1, b1, bt, c1, d1, fin,
-    ohot, band_z, lhs, wz_rhs, plane, pick, pzt, recip,
+    a1, b1, bt, c1, d1, fin, table, tables,
+    ohot, band_z, lhs, wz_rhs, near_rhs, plane, plane_z, pad_x, pad_y, pad_z, pick, pzt, recip,
     in_sem, small_sem, first_send, first_recv, halo_send, halo_recv, row_send, row_recv, vouched,
+    table_send, table_recv,
 ):
     gx = lax.axis_index("gx")
     gy = lax.axis_index("gy")
@@ -135,6 +136,10 @@
         return carry
 
     lax.fori_loop(0, NV, clear, 0)
+    for pad in (pad_x, pad_y, pad_z):
+        size = pad.shape[0]
+        pad[0:8] = jnp.zeros((8, SLOTS), F32)
+        pad[size - 8 : size] = jnp.zeros((8, SLOTS), F32)
 
     z_from = lax.broadcasted_iota(jnp.int32, (CZ, CZ), 0)
     z_to = lax.broadcasted_iota(jnp.int32, (CZ, CZ), 1)
@@ -207,6 +212,7 @@
             halo = (hx, hx, hy, hy)[side]
             for step in range(STEPS):
                 halo[step, side % 2] = jnp.zeros(halo.shape[2:], F32)
+            tables[side] = jnp.zeros((32, SLOTS), F32)
 
     def pack_faces(step, v):
         flat = (g0, g1)[step].reshape(NV * PX * PY, CZ)
@@ -313,29 +319,49 @@
     lax.fori_loop(0, NV, first_lhs, 0)
 
     rows_wait(c1, DEVICES - GX, row_recv.at[1])
-    table = jnp.transpose(c1[...])
-    asked = jnp.concatenate([table[0:32], table[32:64]], axis=1)
-    wx = asked[0:8]
-    wy = asked[8:16]
-    wz = asked[16:24]
+    turned = jnp.transpose(c1[...])
+    table[:, 0:DEVICES] = turned[0:32]
+    table[:, DEVICES:] = turned[32:64]
+
+    def table_copy(side):
+        return pltpu.make_async_remote_copy(
+            src_ref=table, dst_ref=tables.at[side],
+            send_sem=table_send.at[side], recv_sem=table_recv.at[side],
+            device_id=targets[side], device_id_type=MESH,
+        )
+
+    for side in range(4):
+        @pl.when(sends[side])
+        def _():
+            table_copy(side).start()
+
+    row8 = lax.broadcasted_iota(jnp.int32, (8, SLOTS), 0)
+
+    def weights_of(asked):
+        block = asked[29:30].astype(jnp.int32)
+        places = (block // 64, (block // 16) % 4, block % 16)
+        spread = [
+            jnp.concatenate(
+                [jnp.where(place == b, asked[8 * d : 8 * d + 8], 0.0) for b in range(size // 8)],
+                axis=0,
+            )
+            for d, (place, size) in enumerate(zip(places, (CX, CY, CZ)))
+        ]
+        return places, spread
+
+    def put_three(ref, at, values):
+        high, low = split(values)
+        ref[0:CZ, at] = high
+        ref[CZ : 2 * CZ, at] = high
+        ref[2 * CZ :, at] = low
+
+    asked = table[...]
+    (kx, ky, kz), (weights_x, weights_y, weights_z) = weights_of(asked)
     last = asked[24:32]
-    block = last[5:6].astype(jnp.int32)
     offset = last[6:7].astype(jnp.int32)
     live = last[7:8]
-    row8 = lax.broadcasted_iota(jnp.int32, (8, SLOTS), 0)
     near = jnp.where(row8 < NV, last, 0.0)
-    kx = block // 64
-    ky = (block // 16) % 4
-    kz = block % 16
-    weights_z = jnp.concatenate(
-        [jnp.where(kz == b, wz, 0.0) for b in range(CZ // 8)], axis=0
-    )
-    z_high, z_low = split(weights_z)
-    wz_rhs[0:CZ] = z_high
-    wz_rhs[CZ : 2 * CZ] = z_high
-    wz_rhs[2 * CZ :] = z_low
-    weights_x = jnp.concatenate([jnp.where(kx == b, wx, 0.0) for b in range(CX // 8)], axis=0)
-    weights_y = jnp.concatenate([jnp.where(ky == b, wy, 0.0) for b in range(CY // 8)], axis=0)
+    put_three(wz_rhs, slice(0, SLOTS), weights_z)
     for x in range(CX):
         plane[x * CY : (x + 1) * CY] = weights_x[x : x + 1] * weights_y
     cell = (8 * kx + offset // 64) * CY + 8 * ky + (offset // 8) % 8
@@ -352,17 +378,33 @@
     )
     recip[...] = 1.0 / (1.0 + counts)
 
+    def moved(pad, values, dim):
+        size = values.shape[0]
+        pad[8 : 8 + size] = values
+        total = jnp.zeros_like(values)
+        for j in OFFSETS:
+            total = total + pad[8 - j : 8 - j + size] * tap(dim, j)
+        return total
+
+    moved_x = weights_x * CENTER + moved(pad_x, weights_x, 0)
+    moved_y = moved(pad_y, weights_y, 1)
+    put_three(wz_rhs, slice(SLOTS, 2 * SLOTS), moved(pad_z, weights_z, 2))
+    for x in range(CX):
+        plane_z[x * CY : (x + 1) * CY] = (
+            moved_x[x : x + 1] * weights_y + weights_x[x : x + 1] * moved_y
+        )
+
     def relaxed(step, near):
         def body(v, interp):
             if step == 0:
-                t = jnp.dot(lhs[variable(v)], wz_rhs[...], preferred_element_type=F32)
+                t = jnp.dot(lhs[variable(v)], wz_rhs[:, 0:SLOTS], preferred_element_type=F32)
             else:
                 for side in range(4):
                     @pl.when(takes[side])
                     def _():
                         face(1, side, v).wait_recv()
                 add_halo(1, v)
-                t = three_term(flat_res[variable(v)], wz_rhs[...])
+                t = three_term(flat_res[variable(v)], wz_rhs[:, 0:SLOTS])
             here = jnp.sum(t * plane[...], axis=0, keepdims=True)
             return jnp.where(row8 == v, here, interp)
 
@@ -387,25 +429,74 @@
     near = relaxed(0, near)
 
     def second_faces(v, carry):
-        g1[v, 3 : 3 + CX, Y0 : Y0 + CY] = injected(v, near)
+        values = injected(v, near)
+        g1[v, 3 : 3 + CX, Y0 : Y0 + CY] = values
         pack_faces(1, v)
         for side in range(4):
             @pl.when(sends[side])
             def _():
                 face(1, side, v).start()
+        high, low = split(values.reshape(CX * CY, CZ))
+        lhs[variable(v), 0:CZ] = high
+        lhs[variable(v), CZ : 2 * CZ] = low
+        lhs[variable(v), 2 * CZ :] = high
         return carry
 
     lax.fori_loop(0, NV, second_faces, 0, unroll=True)
-    interior(1)
-    near = relaxed(1, near)
+
+    def own_part(v, own):
+        t = jnp.dot(lhs[variable(v)], wz_rhs[...], preferred_element_type=F32)
+        both = t[:, 0:SLOTS] * plane_z[...] + t[:, SLOTS:] * plane[...]
+        return jnp.where(row8 == v, jnp.sum(both, axis=0, keepdims=True), own)
+
+    own = lax.fori_loop(0, NV, own_part, jnp.zeros((8, SLOTS), F32), unroll=True)
+    parts = [near + relaxation * (own - near)]
+    for side in range(4):
+        @pl.when(takes[side])
+        def _():
+            table_copy(side).wait_recv()
+        _, spread = weights_of(tables[side])
+        put_three(near_rhs.at[side], slice(0, SLOTS), spread[2])
+        dim = side // 2
+        across, beside = spread[dim], spread[1 - dim]
+        size = across.shape[0]
+        reach = []
+        for i in range(3):
+            total = jnp.zeros((1, SLOTS), F32)
+            for j in range(1, 4):
+                if side % 2 == 0 and j > i:
+                    total = total + across[size + i - j : size + i - j + 1] * tap(dim, j)
+                if side % 2 == 1 and j >= 3 - i:
+                    total = total + across[i - 3 + j : i - 2 + j] * tap(dim, -j)
+            reach.append(total * beside)
+        reach = jnp.concatenate(reach, axis=0)
+        if dim == 0:
+            first = 0 if side == 0 else (CX - 3) * CY
+            left = jnp.concatenate(
+                [lhs[v * CX * CY + first : v * CX * CY + first + 3 * CY] for v in range(NV)], axis=0
+            )
+            t = jnp.dot(left, near_rhs[side], preferred_element_type=F32)
+        else:
+            t = three_term(sy[1, 3 - side].reshape(NV * 3 * CX, CZ), near_rhs[side])
+        rows = reach.shape[0]
+        added = jnp.zeros((8, SLOTS), F32)
+        for v in range(NV):
+            here = jnp.sum(t[v * rows : (v + 1) * rows] * reach, axis=0, keepdims=True)
+            added = jnp.where(row8 == v, here, added)
+        parts.append(relaxation * added)
 
     back = jnp.concatenate(
-        [near[:, :DEVICES], near[:, DEVICES:], jnp.zeros((DEVICES - 16, DEVICES), F32)], axis=0
+        [part[:, half : half + DEVICES] for part in parts for half in (0, DEVICES)]
+        + [jnp.zeros((DEVICES - 80, DEVICES), F32)],
+        axis=0,
     )
     d1[...] = jnp.transpose(back)
     for px, py in others():
         rows_to(d1, py * GX + px, 1, fin, me, 2, (px, py))
     fin[pl.ds(me, 1)] = d1[pl.ds(gy * GX + gx, 1)]
+
+    interior(1)
+    near = relaxed(1, near)
 
     def last_injection(v, carry):
         flow_out[v] = injected(v, near)
@@ -419,6 +510,7 @@
         @pl.when(sends[side])
         def _():
             face(0, side).wait_send()
+            table_copy(side).wait_send()
 
     def drain(v, carry):
         for side in range(4):
@@ -431,9 +523,12 @@
     rows_wait(d1, DEVICES - 1, row_send.at[2])
     rows_wait(fin, DEVICES - 1, row_recv.at[2])
     returned = jnp.transpose(fin[...])
+    total = returned[0:16]
+    for side, shift in enumerate((DEVICES - GY, GY, DEVICES - 1, 1)):
+        total = total + pltpu.roll(returned[16 + 16 * side : 32 + 16 * side], shift, axis=1)
     served = jnp.dot(
-        returned[0:8], ohot[0], precision=HIGHEST, preferred_element_type=F32
-    ) + jnp.dot(returned[8:16], ohot[1], precision=HIGHEST, preferred_element_type=F32)
+        total[0:8], ohot[0], precision=HIGHEST, preferred_element_type=F32
+    ) + jnp.dot(total[8:16], ohot[1], precision=HIGHEST, preferred_element_type=F32)
     near_out[...] = served[0:NV]
 
 
@@ -484,11 +579,18 @@
             vmem((DEVICES, 128), F32),
             vmem((DEVICES, 128), F32),
             vmem((DEVICES, 128), F32),
+            vmem((32, SLOTS), F32),
+            vmem((4, 32, SLOTS), F32),
             vmem((2, DEVICES, FR), F32),
             vmem((3 * CZ, CZ), BF16),
             vmem((NV * CX * CY, 3 * CZ), BF16),
-            vmem((3 * CZ, SLOTS), BF16),
+            vmem((3 * CZ, 2 * SLOTS), BF16),
+            vmem((4, 3 * CZ, SLOTS), BF16),
             vmem((CX * CY, SLOTS), F32),
+            vmem((CX * CY, SLOTS), F32),
+            vmem((CX + 16, SLOTS), F32),
+            vmem((CY + 16, SLOTS), F32),
+            vmem((CZ + 16, SLOTS), F32),
             vmem((CX * CY, SLOTS), BF16),
             vmem((CZ, 2 * SLOTS), BF16),
             vmem((CX * CY, CZ), F32),
@@ -501,6 +603,8 @@
             dma((3,)),
             dma((3,)),
             pltpu.SemaphoreType.REGULAR,
+            dma((4,)),
+            dma((4,)),
         ],
         compiler_params=pltpu.CompilerParams(
             collective_id=0, has_side_effects=True, vmem_limit_bytes=40 * 1024 * 1024

time: 32.3 us -> 30.6 us (0.947)
  Pallas kernels: 31.6 us -> 29.8 us
    pallas_call x1, Pallas kernels: 30.5 us -> 28.7 us  [shards(): pl.pallas_call(kernel, out_shape=(vmem((NV, CX, CY, CZ), F32), vmem((NV,...]
where the time goes in v6:
time: 30.6 us; the launch traced here: 30.5 us
  Pallas kernels  29.8 us (97%)
  between operations  0.64 us (2%)
    pallas_call x1, Pallas kernels, shards(): pl.pallas_call(kernel, out_shape=(vmem((NV, CX, CY, CZ), F32), vmem((NV,...  28.7 us
    pallas_call x1, Pallas kernels, shards(): pl.pallas_call(hand_over, out_shape=(jax.ShapeDtypeStruct((NV, CX, CY, CZ...  1.08 us

profile of v6, /device:TPU:1, one launch (start us, length us, event | category | flops | bytes accessed | tf_op | source)
XLA Modules:
  0.0 30.5 jit_solution(9898911638701537129)
XLA Ops:
  0.6 28.7 %rotor_wake_steps.1 = (f32[5,16,32,128]{3,2,1,0:T(8,128)S(1)}, f32[5,128]{1,0:T(8,128)S(1)}) custom-call(f32[5,16,32,128]{3,2,1,0:T(8,128)} %flow_hbm.1, f32[5,128]{1,0:T(8,128)} %near_hbm.1, s32[1,128]{1,0:T(1,128)} %bitcast.5, s32[1,128]{1,0:T(1,128)} %bitcast.6, s32[1,128]{1,0:T(1,128)} %bitcast.7, f32[24,128]{1,0:T(8,128)} %bitcast.4), custom_call_target="tpu_custom_call" | custom-call | flops 26214400 | bytes 2621440 | tf_op jit(solution)/shard_map/rotor_wake_steps/pallas_call | solution.py:559
  29.4 1.1 %hand_over.1 = (f32[5,16,32,128]{3,2,1,0:T(8,128)}, f32[5,128]{1,0:T(8,128)}) custom-call(f32[5,16,32,128]{3,2,1,0:T(8,128)S(1)} %get-tuple-element.4.flow_vmem, f32[5,128]{1,0:T(8,128)S(1)} %get-tuple-element.5.near_vmem), custom_call_target="tpu_custom_call" | custom-call | tf_op jit(solution)/shard_map/hand_over/pallas_call | solution.py:619

commit v7 on v6

--- a/solution.py
+++ b/solution.py
@@ -67,7 +67,7 @@
     g0, g1, res, hx, hy, sy,
     near_in, owner_in, block_in, offset_in, weights_in,
     a1, b1, bt, c1, d1, fin, table, tables,
-    ohot, band_z, lhs, wz_rhs, near_rhs, plane, plane_z, pad_x, pad_y, pad_z, pick, pzt, recip,
+    ohot, band_z, lhs, wz_rhs, near_rhs, plane, plane_z, pad_x, pad_y, pad_z, pick, recip,
     in_sem, small_sem, first_send, first_recv, halo_send, halo_recv, row_send, row_recv, vouched,
     table_send, table_recv,
 ):
@@ -301,7 +301,8 @@
                 flat_res[at_high] = high
 
     def variable(v):
-        return pl.ds(pl.multiple_of(v * CX * CY, CX * CY), CX * CY)
+        start = v * CX * CY
+        return pl.ds(start if isinstance(v, int) else pl.multiple_of(start, CX * CY), CX * CY)
 
     for side in range(4):
         @pl.when(takes[side])
@@ -368,13 +369,13 @@
     cell = jnp.where(live > 0.5, cell, -1)
     cell_z = 8 * kz + offset % 8
     places = lax.broadcasted_iota(jnp.int32, (CX * CY, SLOTS), 0)
-    pick[...] = jnp.where(places == cell, 1.0, 0.0).astype(F32).astype(BF16)
+    picked = jnp.where(places == cell, 1.0, 0.0).astype(F32).astype(BF16)
+    pick[:, 0:SLOTS] = picked
+    pick[:, SLOTS:] = picked
     places_z = lax.broadcasted_iota(jnp.int32, (CZ, SLOTS), 0)
     hot_z = jnp.where(places_z == cell_z, 1.0, 0.0).astype(F32).astype(BF16)
-    pzt[:, 0:SLOTS] = hot_z
-    pzt[:, SLOTS:] = hot_z
     counts = lax.dot_general(
-        pick[...], hot_z, contract_last, preferred_element_type=F32
+        picked, hot_z, contract_last, preferred_element_type=F32
     )
     recip[...] = 1.0 / (1.0 + counts)
 
@@ -411,25 +412,30 @@
         interp = lax.fori_loop(0, NV, body, jnp.zeros((8, SLOTS), F32), unroll=True)
         return near + relaxation * (interp - near)
 
-    def injected(v, near):
-        here = jnp.sum(jnp.where(row8 == v, near, 0.0), axis=0, keepdims=True)
-        here = jnp.broadcast_to(here, (16, SLOTS))
-        high, low = split(here)
-        hot = pick[...].reshape(CX * CY // 16, 16, SLOTS)
-        left = jnp.concatenate(
-            [
-                (hot * high[None]).reshape(CX * CY, SLOTS),
-                (hot * low[None]).reshape(CX * CY, SLOTS),
-            ],
-            axis=1,
+    def injected(near):
+        right = []
+        for v in range(NV):
+            high, low = split(jnp.broadcast_to(near[v : v + 1], (16, SLOTS)))
+            hot = hot_z.reshape(CZ // 16, 16, SLOTS)
+            right.append(
+                jnp.concatenate(
+                    [
+                        (hot * high[None]).reshape(CZ, SLOTS),
+                        (hot * low[None]).reshape(CZ, SLOTS),
+                    ],
+                    axis=1,
+                )
+            )
+        gained = lax.dot_general(
+            pick[...], jnp.concatenate(right, axis=0), contract_last, preferred_element_type=F32
         )
-        gained = lax.dot_general(left, pzt[...], contract_last, preferred_element_type=F32)
-        return ((flat_res[variable(v)] + gained) * recip[...]).reshape(CX, CY, CZ)
+        for v in range(NV):
+            part = gained[:, v * CZ : (v + 1) * CZ]
+            yield v, ((flat_res[variable(v)] + part) * recip[...]).reshape(CX, CY, CZ)
 
     near = relaxed(0, near)
 
-    def second_faces(v, carry):
-        values = injected(v, near)
+    for v, values in injected(near):
         g1[v, 3 : 3 + CX, Y0 : Y0 + CY] = values
         pack_faces(1, v)
         for side in range(4):
@@ -440,9 +446,6 @@
         lhs[variable(v), 0:CZ] = high
         lhs[variable(v), CZ : 2 * CZ] = low
         lhs[variable(v), 2 * CZ :] = high
-        return carry
-
-    lax.fori_loop(0, NV, second_faces, 0, unroll=True)
 
     def own_part(v, own):
         t = jnp.dot(lhs[variable(v)], wz_rhs[...], preferred_element_type=F32)
@@ -498,11 +501,8 @@
     interior(1)
     near = relaxed(1, near)
 
-    def last_injection(v, carry):
-        flow_out[v] = injected(v, near)
-        return carry
-
-    lax.fori_loop(0, NV, last_injection, 0, unroll=True)
+    for v, values in injected(near):
+        flow_out[v] = values
 
     rows_wait(a1, DEVICES - GY, row_send.at[0])
     rows_wait(bt, DEVICES - GX, row_send.at[1])
@@ -527,8 +527,9 @@
     for side, shift in enumerate((DEVICES - GY, GY, DEVICES - 1, 1)):
         total = total + pltpu.roll(returned[16 + 16 * side : 32 + 16 * side], shift, axis=1)
     served = jnp.dot(
-        total[0:8], ohot[0], precision=HIGHEST, preferred_element_type=F32
-    ) + jnp.dot(total[8:16], ohot[1], precision=HIGHEST, preferred_element_type=F32)
+        jnp.concatenate([total[0:8], total[8:16]], axis=1), ohot[...].reshape(2 * DEVICES, FR),
+        precision=HIGHEST, preferred_element_type=F32,
+    )
     near_out[...] = served[0:NV]
 
 
@@ -591,8 +592,7 @@
             vmem((CX + 16, SLOTS), F32),
             vmem((CY + 16, SLOTS), F32),
             vmem((CZ + 16, SLOTS), F32),
-            vmem((CX * CY, SLOTS), BF16),
-            vmem((CZ, 2 * SLOTS), BF16),
+            vmem((CX * CY, 2 * SLOTS), BF16),
             vmem((CX * CY, CZ), F32),
             dma((NV,)),
             dma((5,)),

time: 30.6 us -> 29.8 us (0.974)
  Pallas kernels: 29.8 us -> 29 us
    pallas_call x1, Pallas kernels: 28.7 us -> 27.9 us  [shards(): pl.pallas_call(kernel, out_shape=(vmem((NV, CX, CY, CZ), F32), vmem((NV,...]
where the time goes in v7:
time: 29.8 us; the launch traced here: 29.7 us
  Pallas kernels  29 us (97%)
  between operations  0.64 us (2%)
    pallas_call x1, Pallas kernels, shards(): pl.pallas_call(kernel, out_shape=(vmem((NV, CX, CY, CZ), F32), vmem((NV,...  27.9 us
    pallas_call x1, Pallas kernels, shards(): pl.pallas_call(hand_over, out_shape=(jax.ShapeDtypeStruct((NV, CX, CY, CZ...  1.08 us

profile of v7, /device:TPU:1, one launch (start us, length us, event | category | flops | bytes accessed | tf_op | source)
XLA Modules:
  0.0 29.7 jit_solution(18123253619432050308)
XLA Ops:
  0.6 27.9 %rotor_wake_steps.1 = (f32[5,16,32,128]{3,2,1,0:T(8,128)S(1)}, f32[5,128]{1,0:T(8,128)S(1)}) custom-call(f32[5,16,32,128]{3,2,1,0:T(8,128)} %flow_hbm.1, f32[5,128]{1,0:T(8,128)} %near_hbm.1, s32[1,128]{1,0:T(1,128)} %bitcast.5, s32[1,128]{1,0:T(1,128)} %bitcast.6, s32[1,128]{1,0:T(1,128)} %bitcast.7, f32[24,128]{1,0:T(8,128)} %bitcast.4), custom_call_target="tpu_custom_call" | custom-call | flops 26214400 | bytes 2621440 | tf_op jit(solution)/shard_map/rotor_wake_steps/pallas_call | solution.py:560
  28.6 1.1 %hand_over.1 = (f32[5,16,32,128]{3,2,1,0:T(8,128)}, f32[5,128]{1,0:T(8,128)}) custom-call(f32[5,16,32,128]{3,2,1,0:T(8,128)S(1)} %get-tuple-element.4.flow_vmem, f32[5,128]{1,0:T(8,128)S(1)} %get-tuple-element.5.near_vmem), custom_call_target="tpu_custom_call" | custom-call | tf_op jit(solution)/shard_map/hand_over/pallas_call | solution.py:619

commit v8 on v7

--- a/solution.py
+++ b/solution.py
@@ -67,8 +67,8 @@
     g0, g1, res, hx, hy, sy,
     near_in, owner_in, block_in, offset_in, weights_in,
     a1, b1, bt, c1, d1, fin, table, tables,
-    ohot, band_z, lhs, wz_rhs, near_rhs, plane, plane_z, pad_x, pad_y, pad_z, pick, recip,
-    in_sem, small_sem, first_send, first_recv, halo_send, halo_recv, row_send, row_recv, vouched,
+    ohot, ohot_low, band_z, lhs, wz_rhs, near_rhs, plane, plane_z, pad_x, pad_y, pad_z, pick, recip,
+    in_sem, small_sem, halo_send, halo_recv, row_send, row_recv, vouched,
     table_send, table_recv,
 ):
     gx = lax.axis_index("gx")
@@ -77,17 +77,21 @@
     chip_x, core = gx // 2, lax.rem(gx, 2)
     chip_z, chip_y = gy // 4, lax.rem(gy, 4)
 
-    def others():
-        for dx, dc, dz, dy in OTHERS:
-            yield (
+    placed = [
+        (
+            (dx, dc, dz, dy),
+            (
                 lax.rem(chip_x + dx, 4) * 2 + lax.rem(core + dc, 2),
                 lax.rem(chip_z + dz, 4) * 4 + lax.rem(chip_y + dy, 4),
-            )
-
-    along_x = [(lax.rem(gx + k, GX), gy) for k in range(1, GX)]
-    along_y = [(gx, chip_z * 4 + lax.rem(chip_y + k, 4)) for k in range(1, 4)]
-    along_z = [(gx, lax.rem(gy + 4 * k, GY)) for k in range(1, 4)]
-    plane_yz = [(gx, lax.rem(gy + k, GY)) for k in range(1, GY)]
+            ),
+        )
+        for dx, dc, dz, dy in OTHERS
+    ]
+
+    along_x = [(px, py) for o, (px, py) in placed if o[2] == o[3] == 0]
+    along_y = [(gx, py) for o, (px, py) in placed if o[0] == o[1] == o[2] == 0]
+    along_z = [(gx, py) for o, (px, py) in placed if o[0] == o[1] == o[3] == 0]
+    plane_yz = [(gx, py) for o, (px, py) in placed if o[0] == o[1] == 0]
     barrier = pltpu.get_barrier_semaphore()
     for peer in along_y + along_z + along_x:
         pl.semaphore_signal(barrier, inc=1, device_id=peer, device_id_type=MESH)
@@ -162,6 +166,7 @@
     mine = owner_wide == row
     ohot[0] = jnp.where(mine & (rank < 0.5), 1.0, 0.0).astype(F32)
     ohot[1] = jnp.where(mine & (rank > 0.5), 1.0, 0.0).astype(F32)
+    ohot_low[...] = ohot[...].reshape(2 * DEVICES, FR).astype(BF16)
     payload = jnp.concatenate(
         [
             weights_in[...],
@@ -187,22 +192,15 @@
     sends = (gx < GX - 1, gx > 0, gy < GY - 1, gy > 0)
     takes = (gx > 0, gx < GX - 1, gy > 0, gy < GY - 1)
 
-    def face(step, side, v=None):
-        g = (g0, g1)[step]
+    def face(step, side):
         if side < 2:
             layers = pl.ds(CX if side == 0 else 3, 3)
-            if v is None:
-                src, dst = g.at[:, layers, pl.ds(Y0, CY)], hx.at[step, side]
-            else:
-                src, dst = g.at[v, layers, pl.ds(Y0, CY)], hx.at[step, side, v]
-        elif v is None:
+            src, dst = (g0, g1)[step].at[:, layers, pl.ds(Y0, CY)], hx.at[step, side]
+        else:
             src, dst = sy.at[step, side - 2], hy.at[step, side - 2]
-        else:
-            src, dst = sy.at[step, side - 2, v], hy.at[step, side - 2, v]
         return pltpu.make_async_remote_copy(
             src_ref=src, dst_ref=dst,
-            send_sem=first_send.at[side] if v is None else halo_send.at[v, side],
-            recv_sem=first_recv.at[side] if v is None else halo_recv.at[v, side],
+            send_sem=halo_send.at[step, side], recv_sem=halo_recv.at[step, side],
             device_id=targets[side], device_id_type=MESH,
         )
 
@@ -258,10 +256,10 @@
     x_rows = pl.ds(pl.multiple_of(gx * GY, GY), GY)
     b1[x_rows] = a1[x_rows]
     pl.semaphore_wait(barrier, greeted)
+    for peer in along_y:
+        pl.semaphore_signal(vouched, inc=1, device_id=peer, device_id_type=MESH)
     for peer in along_x:
         rows_to(a1, pl.multiple_of(peer[0] * GY, GY), GY, b1, pl.multiple_of(gx * GY, GY), 0, peer)
-    for peer in along_y:
-        pl.semaphore_signal(vouched, inc=1, device_id=peer, device_id_type=MESH)
     for side in range(4):
         @pl.when(sends[side])
         def _():
@@ -400,15 +398,16 @@
             if step == 0:
                 t = jnp.dot(lhs[variable(v)], wz_rhs[:, 0:SLOTS], preferred_element_type=F32)
             else:
-                for side in range(4):
-                    @pl.when(takes[side])
-                    def _():
-                        face(1, side, v).wait_recv()
                 add_halo(1, v)
                 t = three_term(flat_res[variable(v)], wz_rhs[:, 0:SLOTS])
             here = jnp.sum(t * plane[...], axis=0, keepdims=True)
             return jnp.where(row8 == v, here, interp)
 
+        if step == 1:
+            for side in range(4):
+                @pl.when(takes[side])
+                def _():
+                    face(1, side).wait_recv()
         interp = lax.fori_loop(0, NV, body, jnp.zeros((8, SLOTS), F32), unroll=True)
         return near + relaxation * (interp - near)
 
@@ -438,14 +437,14 @@
     for v, values in injected(near):
         g1[v, 3 : 3 + CX, Y0 : Y0 + CY] = values
         pack_faces(1, v)
-        for side in range(4):
-            @pl.when(sends[side])
-            def _():
-                face(1, side, v).start()
         high, low = split(values.reshape(CX * CY, CZ))
         lhs[variable(v), 0:CZ] = high
         lhs[variable(v), CZ : 2 * CZ] = low
         lhs[variable(v), 2 * CZ :] = high
+    for side in range(4):
+        @pl.when(sends[side])
+        def _():
+            face(1, side).start()
 
     def own_part(v, own):
         t = jnp.dot(lhs[variable(v)], wz_rhs[...], preferred_element_type=F32)
@@ -458,6 +457,7 @@
         @pl.when(takes[side])
         def _():
             table_copy(side).wait_recv()
+    for side in range(4):
         _, spread = weights_of(tables[side])
         put_three(near_rhs.at[side], slice(0, SLOTS), spread[2])
         dim = side // 2
@@ -494,7 +494,7 @@
         axis=0,
     )
     d1[...] = jnp.transpose(back)
-    for px, py in others():
+    for _, (px, py) in placed:
         rows_to(d1, py * GX + px, 1, fin, me, 2, (px, py))
     fin[pl.ds(me, 1)] = d1[pl.ds(gy * GX + gx, 1)]
 
@@ -510,27 +510,23 @@
         @pl.when(sends[side])
         def _():
             face(0, side).wait_send()
+            face(1, side).wait_send()
             table_copy(side).wait_send()
 
-    def drain(v, carry):
-        for side in range(4):
-            @pl.when(sends[side])
-            def _():
-                face(1, side, v).wait_send()
-        return carry
-
-    lax.fori_loop(0, NV, drain, 0)
     rows_wait(d1, DEVICES - 1, row_send.at[2])
     rows_wait(fin, DEVICES - 1, row_recv.at[2])
     returned = jnp.transpose(fin[...])
     total = returned[0:16]
     for side, shift in enumerate((DEVICES - GY, GY, DEVICES - 1, 1)):
         total = total + pltpu.roll(returned[16 + 16 * side : 32 + 16 * side], shift, axis=1)
+    total = jnp.concatenate([total[0:8], total[8:16]], axis=1)
+    high, low = split(total)
+    rest = total - high.astype(F32) - low.astype(F32)
     served = jnp.dot(
-        jnp.concatenate([total[0:8], total[8:16]], axis=1), ohot[...].reshape(2 * DEVICES, FR),
-        precision=HIGHEST, preferred_element_type=F32,
-    )
-    near_out[...] = served[0:NV]
+        jnp.concatenate([high.astype(F32), low.astype(F32), rest], axis=0).astype(BF16),
+        ohot_low[...], preferred_element_type=F32,
+    )
+    near_out[...] = (served[0:8] + served[8:16] + served[16:24])[0:NV]
 
 
 def hand_over(flow_vmem, near_vmem, flow_out, near_out, sems):
@@ -583,6 +579,7 @@
             vmem((32, SLOTS), F32),
             vmem((4, 32, SLOTS), F32),
             vmem((2, DEVICES, FR), F32),
+            vmem((2 * DEVICES, FR), BF16),
             vmem((3 * CZ, CZ), BF16),
             vmem((NV * CX * CY, 3 * CZ), BF16),
             vmem((3 * CZ, 2 * SLOTS), BF16),
@@ -596,10 +593,8 @@
             vmem((CX * CY, CZ), F32),
             dma((NV,)),
             dma((5,)),
-            dma((4,)),
-            dma((4,)),
-            dma((NV, 4)),
-            dma((NV, 4)),
+            dma((STEPS, 4)),
+            dma((STEPS, 4)),
             dma((3,)),
             dma((3,)),
             pltpu.SemaphoreType.REGULAR,

time: 29.8 us -> 28.7 us (0.963)
  Pallas kernels: 29 us -> 28 us
    pallas_call x1, Pallas kernels: 27.9 us -> 26.9 us  [shards(): pl.pallas_call(kernel, out_shape=(vmem((NV, CX, CY, CZ), F32), vmem((NV,...]
where the time goes in v8:
time: 28.7 us; the launch traced here: 28.6 us
  Pallas kernels  28 us (98%)
  between operations  0.64 us (2%)
    pallas_call x1, Pallas kernels, shards(): pl.pallas_call(kernel, out_shape=(vmem((NV, CX, CY, CZ), F32), vmem((NV,...  26.9 us
    pallas_call x1, Pallas kernels, shards(): pl.pallas_call(hand_over, out_shape=(jax.ShapeDtypeStruct((NV, CX, CY, CZ...  1.08 us

profile of v8, /device:TPU:1, one launch (start us, length us, event | category | flops | bytes accessed | tf_op | source)
XLA Modules:
  0.0 28.6 jit_solution(4363907815132047355)
XLA Ops:
  0.6 26.9 %rotor_wake_steps.1 = (f32[5,16,32,128]{3,2,1,0:T(8,128)S(1)}, f32[5,128]{1,0:T(8,128)S(1)}) custom-call(f32[5,16,32,128]{3,2,1,0:T(8,128)} %flow_hbm.1, f32[5,128]{1,0:T(8,128)} %near_hbm.1, s32[1,128]{1,0:T(1,128)} %bitcast.5, s32[1,128]{1,0:T(1,128)} %bitcast.6, s32[1,128]{1,0:T(1,128)} %bitcast.7, f32[24,128]{1,0:T(8,128)} %bitcast.4), custom_call_target="tpu_custom_call" | custom-call | flops 26214400 | bytes 2621440 | tf_op jit(solution)/shard_map/rotor_wake_steps/pallas_call | solution.py:556
  27.5 1.1 %hand_over.1 = (f32[5,16,32,128]{3,2,1,0:T(8,128)}, f32[5,128]{1,0:T(8,128)}) custom-call(f32[5,16,32,128]{3,2,1,0:T(8,128)S(1)} %get-tuple-element.4.flow_vmem, f32[5,128]{1,0:T(8,128)S(1)} %get-tuple-element.5.near_vmem), custom_call_target="tpu_custom_call" | custom-call | tf_op jit(solution)/shard_map/hand_over/pallas_call | solution.py:614

commit v9 on v8

--- a/solution.py
+++ b/solution.py
@@ -130,30 +130,6 @@
 
     for v in range(NV):
         flow_in(v).start()
-
-    def clear(v, carry):
-        for g in (g0, g1):
-            g[v, 0:3, Y0 : Y0 + CY] = jnp.zeros((3, CY, CZ), F32)
-            g[v, PX - 3 : PX, Y0 : Y0 + CY] = jnp.zeros((3, CY, CZ), F32)
-            g[v, 3 : PX - 3, 0:Y0] = jnp.zeros((CX, Y0, CZ), F32)
-            g[v, 3 : PX - 3, Y0 + CY : PY] = jnp.zeros((CX, PY - Y0 - CY, CZ), F32)
-        return carry
-
-    lax.fori_loop(0, NV, clear, 0)
-    for pad in (pad_x, pad_y, pad_z):
-        size = pad.shape[0]
-        pad[0:8] = jnp.zeros((8, SLOTS), F32)
-        pad[size - 8 : size] = jnp.zeros((8, SLOTS), F32)
-
-    z_from = lax.broadcasted_iota(jnp.int32, (CZ, CZ), 0)
-    z_to = lax.broadcasted_iota(jnp.int32, (CZ, CZ), 1)
-    band = jnp.zeros((CZ, CZ), F32)
-    for j in OFFSETS:
-        band = jnp.where(z_from - z_to == j, tap(2, j), band)
-    band_high, band_low = split(band)
-    band_z[0:CZ] = band_high
-    band_z[CZ : 2 * CZ] = band_high
-    band_z[2 * CZ :] = band_low
 
     for copy in small:
         copy.wait()
@@ -204,14 +180,6 @@
             device_id=targets[side], device_id_type=MESH,
         )
 
-    for side in range(4):
-        @pl.when(jnp.logical_not(takes[side]))
-        def _():
-            halo = (hx, hx, hy, hy)[side]
-            for step in range(STEPS):
-                halo[step, side % 2] = jnp.zeros(halo.shape[2:], F32)
-            tables[side] = jnp.zeros((32, SLOTS), F32)
-
     def pack_faces(step, v):
         flat = (g0, g1)[step].reshape(NV * PX * PY, CZ)
         for side, first in ((0, CY - 3), (1, 0)):
@@ -247,12 +215,6 @@
         part = buf.at[pl.ds(0, count)]
         pltpu.make_async_copy(part, part, sem).wait()
 
-    def first_faces(v, carry):
-        flow_in(v).wait()
-        pack_faces(0, v)
-        return carry
-
-    lax.fori_loop(0, NV, first_faces, 0)
     x_rows = pl.ds(pl.multiple_of(gx * GY, GY), GY)
     b1[x_rows] = a1[x_rows]
     pl.semaphore_wait(barrier, greeted)
@@ -260,10 +222,50 @@
         pl.semaphore_signal(vouched, inc=1, device_id=peer, device_id_type=MESH)
     for peer in along_x:
         rows_to(a1, pl.multiple_of(peer[0] * GY, GY), GY, b1, pl.multiple_of(gx * GY, GY), 0, peer)
+
+    def first_faces(v, carry):
+        flow_in(v).wait()
+        pack_faces(0, v)
+        return carry
+
+    lax.fori_loop(0, NV, first_faces, 0)
     for side in range(4):
         @pl.when(sends[side])
         def _():
             face(0, side).start()
+
+    for side in range(4):
+        @pl.when(jnp.logical_not(takes[side]))
+        def _():
+            halo = (hx, hx, hy, hy)[side]
+            for step in range(STEPS):
+                halo[step, side % 2] = jnp.zeros(halo.shape[2:], F32)
+            tables[side] = jnp.zeros((32, SLOTS), F32)
+
+    def clear(v, carry):
+        for g in (g0, g1):
+            g[v, 0:3, Y0 : Y0 + CY] = jnp.zeros((3, CY, CZ), F32)
+            g[v, PX - 3 : PX, Y0 : Y0 + CY] = jnp.zeros((3, CY, CZ), F32)
+            g[v, 3 : PX - 3, 0:Y0] = jnp.zeros((CX, Y0, CZ), F32)
+            g[v, 3 : PX - 3, Y0 + CY : PY] = jnp.zeros((CX, PY - Y0 - CY, CZ), F32)
+        return carry
+
+    lax.fori_loop(0, NV, clear, 0)
+    for pad in (pad_x, pad_y, pad_z):
+        size = pad.shape[0]
+        pad[0:8] = jnp.zeros((8, SLOTS), F32)
+        pad[size - 8 : size] = jnp.zeros((8, SLOTS), F32)
+
+    z_from = lax.broadcasted_iota(jnp.int32, (CZ, CZ), 0)
+    z_to = lax.broadcasted_iota(jnp.int32, (CZ, CZ), 1)
+    band = jnp.zeros((CZ, CZ), F32)
+    for j in OFFSETS:
+        band = jnp.where(z_from - z_to == j, tap(2, j), band)
+    band_high, band_low = split(band)
+    band_z[0:CZ] = band_high
+    band_z[CZ : 2 * CZ] = band_high
+    band_z[2 * CZ :] = band_low
+
     interior(0)
     rows_wait(b1, DEVICES - GY, row_recv.at[0])
     for h in range(GY):
@@ -329,7 +331,7 @@
             device_id=targets[side], device_id_type=MESH,
         )
 
-    for side in range(4):
+    for side in (2, 3, 0, 1):
         @pl.when(sends[side])
         def _():
             table_copy(side).start()
@@ -454,10 +456,11 @@
     own = lax.fori_loop(0, NV, own_part, jnp.zeros((8, SLOTS), F32), unroll=True)
     parts = [near + relaxation * (own - near)]
     for side in range(4):
-        @pl.when(takes[side])
-        def _():
-            table_copy(side).wait_recv()
-    for side in range(4):
+        if side % 2 == 0:
+            for other in (side, side + 1):
+                @pl.when(takes[other])
+                def _():
+                    table_copy(other).wait_recv()
         _, spread = weights_of(tables[side])
         put_three(near_rhs.at[side], slice(0, SLOTS), spread[2])
         dim = side // 2

time: 28.7 us -> 28.4 us (0.990)
  Pallas kernels: 28 us -> 27.7 us
    pallas_call x1, Pallas kernels: 26.9 us -> 26.6 us  [shards(): pl.pallas_call(kernel, out_shape=(vmem((NV, CX, CY, CZ), F32), vmem((NV,...]
where the time goes in v9:
time: 28.4 us; the launch traced here: 28.3 us
  Pallas kernels  27.7 us (98%)
  between operations  0.64 us (2%)
    pallas_call x1, Pallas kernels, shards(): pl.pallas_call(kernel, out_shape=(vmem((NV, CX, CY, CZ), F32), vmem((NV,...  26.6 us
    pallas_call x1, Pallas kernels, shards(): pl.pallas_call(hand_over, out_shape=(jax.ShapeDtypeStruct((NV, CX, CY, CZ...  1.08 us

profile of v9, /device:TPU:1, one launch (start us, length us, event | category | flops | bytes accessed | tf_op | source)
XLA Modules:
  0.0 28.3 jit_solution(11289707408946494667)
XLA Ops:
  0.6 26.6 %rotor_wake_steps.1 = (f32[5,16,32,128]{3,2,1,0:T(8,128)S(1)}, f32[5,128]{1,0:T(8,128)S(1)}) custom-call(f32[5,16,32,128]{3,2,1,0:T(8,128)} %flow_hbm.1, f32[5,128]{1,0:T(8,128)} %near_hbm.1, s32[1,128]{1,0:T(1,128)} %bitcast.5, s32[1,128]{1,0:T(1,128)} %bitcast.6, s32[1,128]{1,0:T(1,128)} %bitcast.7, f32[24,128]{1,0:T(8,128)} %bitcast.4), custom_call_target="tpu_custom_call" | custom-call | flops 26214400 | bytes 2621440 | tf_op jit(solution)/shard_map/rotor_wake_steps/pallas_call | solution.py:559
  27.2 1.1 %hand_over.1 = (f32[5,16,32,128]{3,2,1,0:T(8,128)}, f32[5,128]{1,0:T(8,128)}) custom-call(f32[5,16,32,128]{3,2,1,0:T(8,128)S(1)} %get-tuple-element.4.flow_vmem, f32[5,128]{1,0:T(8,128)S(1)} %get-tuple-element.5.near_vmem), custom_call_target="tpu_custom_call" | custom-call | tf_op jit(solution)/shard_map/hand_over/pallas_call | solution.py:617

commit v10 on v9

--- a/solution.py
+++ b/solution.py
@@ -93,7 +93,7 @@
     along_z = [(gx, py) for o, (px, py) in placed if o[0] == o[1] == o[3] == 0]
     plane_yz = [(gx, py) for o, (px, py) in placed if o[0] == o[1] == 0]
     barrier = pltpu.get_barrier_semaphore()
-    for peer in along_y + along_z + along_x:
+    for peer in along_z + along_y + along_x:
         pl.semaphore_signal(barrier, inc=1, device_id=peer, device_id_type=MESH)
     after = (chip_y == 3) & (gy < GY - 1)
     before = (chip_y == 0) & (gy > 0)

time: 28.4 us -> 28.4 us (level)
  no operation moved by 1% of the time
where the time goes in v10:
time: 28.4 us; the launch traced here: 28.3 us
  Pallas kernels  27.6 us (97%)
  between operations  0.64 us (2%)
    pallas_call x1, Pallas kernels, shards(): pl.pallas_call(kernel, out_shape=(vmem((NV, CX, CY, CZ), F32), vmem((NV,...  26.6 us
    pallas_call x1, Pallas kernels, shards(): pl.pallas_call(hand_over, out_shape=(jax.ShapeDtypeStruct((NV, CX, CY, CZ...  1.08 us

profile of v10, /device:TPU:1, one launch (start us, length us, event | category | flops | bytes accessed | tf_op | source)
XLA Modules:
  0.0 28.3 jit_solution(17412994115583608531)
XLA Ops:
  0.6 26.6 %rotor_wake_steps.1 = (f32[5,16,32,128]{3,2,1,0:T(8,128)S(1)}, f32[5,128]{1,0:T(8,128)S(1)}) custom-call(f32[5,16,32,128]{3,2,1,0:T(8,128)} %flow_hbm.1, f32[5,128]{1,0:T(8,128)} %near_hbm.1, s32[1,128]{1,0:T(1,128)} %bitcast.5, s32[1,128]{1,0:T(1,128)} %bitcast.6, s32[1,128]{1,0:T(1,128)} %bitcast.7, f32[24,128]{1,0:T(8,128)} %bitcast.4), custom_call_target="tpu_custom_call" | custom-call | flops 26214400 | bytes 2621440 | tf_op jit(solution)/shard_map/rotor_wake_steps/pallas_call | solution.py:559
  27.2 1.1 %hand_over.1 = (f32[5,16,32,128]{3,2,1,0:T(8,128)}, f32[5,128]{1,0:T(8,128)}) custom-call(f32[5,16,32,128]{3,2,1,0:T(8,128)S(1)} %get-tuple-element.4.flow_vmem, f32[5,128]{1,0:T(8,128)S(1)} %get-tuple-element.5.near_vmem), custom_call_target="tpu_custom_call" | custom-call | tf_op jit(solution)/shard_map/hand_over/pallas_call | solution.py:617
